TPU v7x, 32 devices: a whole 2x2x4 slice. The times are simulated.
32 devices in a mesh: seq: 16 (over z, y, x), tp: 2 (over core).
Axes of the slice: x: 2, y: 2, z: 4, core: 2. Of those that a mesh axis runs over, the one named last changes fastest.
Arguments:
- residual_in: bfloat16 [4096, 8192], P('seq', 'tp'), may hold values from -6 to 6
- features: bfloat16 [3, 4096, 8192], P(None, 'seq', 'tp'), may hold values from -6 to 6
- short_mr: float32 [3, 7, 8192], P(None, None, 'tp'), may hold values from -2 to 2
- medium: bfloat16 [128, 512], P(None, 'tp'), may hold values from -0.5 to 0.5
- skip_mr: float32 [8192], P('tp'), may hold values from 0.5 to 1.5
- li_gates: bfloat16 [2, 4096, 8192], P(None, 'seq', 'tp'), may hold values from -6 to 6
- short_li: float32 [3, 7, 8192], P(None, None, 'tp'), may hold values from -2 to 2
- poles: float32 [16, 8192], P(None, 'tp'), may hold values from 0 to 1, as said below
- residues: float32 [16, 8192], P(None, 'tp'), may hold values from -0.5 to 0.5
- skip_li: float32 [8192], P('tp'), may hold values from 0.5 to 1.5
- w_out: bfloat16 [8192, 8192], P('seq', 'tp'), may hold values from -0.0625 to 0.0625
Outputs:
- block_out: bfloat16 [4096, 8192], P('seq', 'tp')
Inputs may be any that keep to these rules, and one draw needn't show every extreme that they name: `poles`: every pole lies strictly between 0 and 1.
All inputs are finite; a program needn't handle non-finite values.
Results may differ from a plain program's by a relative error of at most 0.0064.
Values may be sent and summed in bfloat16 or wider, within the bound.
A program may use at most 384 MiB of HBM per device.

v0:
```python
import functools
import jax
import jax.numpy as jnp
from jax import lax
from jax.experimental import pallas as pl
from jax.experimental.pallas import tpu as pltpu
from jax.sharding import PartitionSpec as P

rim = 8
inner = 4
f32 = jnp.float32
bf16 = jnp.bfloat16


def from_behind(value, axis, steps):
    count = lax.axis_size(axis)
    return lax.ppermute(value, axis, [(source, source + steps) for source in range(count - steps)])


def params():
    return pltpu.CompilerParams(
        dimension_semantics=("arbitrary",), vmem_limit_bytes=48 * 1024 * 1024
    )


def tile_of(channels, most):
    return min(channels, most)


def short_rows(window, taps, rows):
    total = taps[0:1] * window[rim : rim + rows]
    for lag in range(1, taps.shape[0]):
        total = total + taps[lag : lag + 1] * window[rim - lag : rim - lag + rows]
    return total


def window_of(front, main_ref, index, start, rows, lanes):
    if start == 0:
        body = main_ref[index, 0:rows, lanes].astype(f32)
        return jnp.concatenate([front, body], axis=0)
    body = main_ref[index, start - 16 : start + rows, lanes].astype(f32)
    return body[16 - rim :]


def gate_kernel(k_ref, v_ref, front_ref, taps_ref, z_ref, *, step):
    rows = k_ref.shape[1]
    for lane in range(0, k_ref.shape[2], 128):
        lanes = pl.ds(lane, 128)
        for start in range(0, rows, step):
            k_win = window_of(front_ref[1, :, lanes], k_ref, 0, start, step, lanes)
            v_win = window_of(front_ref[2, :, lanes], v_ref, 0, start, step, lanes)
            k_out = short_rows(k_win, taps_ref[1, :, lanes], step)
            v_out = short_rows(v_win, taps_ref[2, :, lanes], step)
            z_ref[pl.ds(start, step), lanes] = (k_out * v_out).astype(bf16)


def medium_kernel(
    q_ref, front_ref, head_ref, main_ref, med_ref, taps_ref, skip_ref, y_ref, win, wide, *, width
):
    rows = main_ref.shape[0]
    reach, groups = med_ref.shape
    lanes_all = main_ref.shape[1]
    win[0:reach] = head_ref[...].astype(f32)
    win[reach:] = main_ref[...].astype(f32)
    base = pl.program_id(0) * lanes_all
    owner = (base + lax.broadcasted_iota(jnp.int32, (groups, lanes_all), 1)) // width
    pick = (owner == lax.broadcasted_iota(jnp.int32, (groups, lanes_all), 0)).astype(bf16)
    wide[...] = jnp.dot(med_ref[...], pick, preferred_element_type=f32)

    @pl.loop(0, lanes_all // 128)
    def _(tile):
        lanes = pl.ds(pl.multiple_of(tile * 128, 128), 128)
        total = None
        for part in range(rim):
            acc = None
            for block in range(reach // rim):
                lag = block * rim + part
                first = reach - rim - block * rim
                term = wide[lag : lag + 1, lanes] * win[first : first + rows + rim, lanes]
                acc = term if acc is None else acc + term
            moved = acc[rim - part : rim - part + rows]
            total = moved if total is None else total + moved
        q_win = jnp.concatenate([front_ref[:, lanes], q_ref[0, :, lanes].astype(f32)], axis=0)
        q_out = short_rows(q_win, taps_ref[0, :, lanes], rows)
        z_one = win[reach : reach + rows, lanes]
        y_ref[:, lanes] = (q_out * (total + skip_ref[:, lanes] * z_one)).astype(bf16)


def states_kernel(
    g_ref, ylo_ref, yhi_ref, front_ref, taps_ref, poles_ref, q_ref, z_ref, end_ref, both, *, step
):
    half = ylo_ref.shape[0]
    rows = 2 * half
    both[0, 0:half] = ylo_ref[...]
    both[0, half:rows] = yhi_ref[...]
    for lane in range(0, g_ref.shape[2], 128):
        lanes = pl.ds(lane, 128)
        for start in range(0, rows, step):
            q_win = window_of(front_ref[0, :, lanes], g_ref, 0, start, step, lanes)
            k_win = window_of(front_ref[1, :, lanes], g_ref, 1, start, step, lanes)
            v_win = window_of(front_ref[2, :, lanes], both, 0, start, step, lanes)
            q_ref[pl.ds(start, step), lanes] = short_rows(q_win, taps_ref[0, :, lanes], step)
            k_out = short_rows(k_win, taps_ref[1, :, lanes], step)
            v_out = short_rows(v_win, taps_ref[2, :, lanes], step)
            z_ref[pl.ds(start, step), lanes] = k_out * v_out
    poles = poles_ref[...]

    def advance(block, state):
        z_rows = z_ref[pl.ds(pl.multiple_of(block * rim, rim), rim), :]
        for row in range(rim):
            state = poles * state + z_rows[row : row + 1]
        return state

    end_ref[...] = lax.fori_loop(0, rows // rim, advance, jnp.zeros_like(poles))


def long_kernel(z_ref, q_ref, in_ref, poles_ref, res_ref, skip_ref, y_ref):
    rows = z_ref.shape[0]
    poles = poles_ref[...]
    residues = res_ref[...]
    skip = skip_ref[...]

    def advance(block, state):
        for part in range(2):
            start = pl.multiple_of(block * 2 * rim + part * rim, rim)
            z_rows = z_ref[pl.ds(start, rim), :]
            outs = []
            for row in range(rim):
                state = poles * state + z_rows[row : row + 1]
                outs.append(jnp.sum(residues * state, axis=0, keepdims=True))
            long_out = jnp.concatenate(outs, axis=0)
            y = q_ref[pl.ds(start, rim), :] * (long_out + skip * z_rows)
            halves = y if part == 0 else jnp.concatenate([halves, y], axis=0)
        y_ref[0, pl.ds(pl.multiple_of(block * 2 * rim, 2 * rim), 2 * rim), :] = halves.astype(bf16)
        return state

    lax.fori_loop(0, rows // (2 * rim), advance, in_ref[...])


def cost(flops, bytes_moved):
    return pl.CostEstimate(flops=flops, bytes_accessed=bytes_moved, transcendentals=0)


def gate(features, front, taps):
    _, rows, channels = features.shape
    ct = tile_of(channels, 256)
    lags = taps.shape[1]
    return pl.pallas_call(
        functools.partial(gate_kernel, step=64),
        grid=(channels // ct,),
        in_specs=[
            pl.BlockSpec((1, rows, ct), lambda i: (1, 0, i)),
            pl.BlockSpec((1, rows, ct), lambda i: (2, 0, i)),
            pl.BlockSpec((3, rim, ct), lambda i: (0, 0, i)),
            pl.BlockSpec((3, lags, ct), lambda i: (0, 0, i)),
        ],
        out_specs=pl.BlockSpec((rows, ct), lambda i: (0, i)),
        out_shape=jax.ShapeDtypeStruct((rows, channels), bf16),
        compiler_params=params(),
        cost_estimate=cost(60 * rows * channels, 6 * rows * channels),
        name="gate",
    )(features, features, front, taps)


def medium(features, part, q_front, head, main, main_part, medium_taps, taps, skip):
    channels = features.shape[2]
    rows = medium_taps.shape[0]
    ct = tile_of(channels, 512)
    lags = taps.shape[1]
    groups = medium_taps.shape[1]
    return pl.pallas_call(
        functools.partial(medium_kernel, width=channels // groups),
        grid=(channels // ct,),
        in_specs=[
            pl.BlockSpec((1, rows, ct), lambda i: (0, part, i)),
            pl.BlockSpec((rim, ct), lambda i: (0, i)),
            pl.BlockSpec((rows, ct), lambda i: (0, i)),
            pl.BlockSpec((rows, ct), lambda i: (main_part, i)),
            pl.BlockSpec((rows, groups), lambda i: (0, 0)),
            pl.BlockSpec((3, lags, ct), lambda i: (0, 0, i)),
            pl.BlockSpec((1, ct), lambda i: (0, i)),
        ],
        out_specs=pl.BlockSpec((rows, ct), lambda i: (0, i)),
        out_shape=jax.ShapeDtypeStruct((rows, channels), bf16),
        scratch_shapes=[pltpu.VMEM((2 * rows, ct), f32), pltpu.VMEM((rows, ct), f32)],
        compiler_params=params(),
        cost_estimate=cost(40000 * rows * channels // 16, 8 * rows * channels),
        name="medium",
    )(features, q_front, head, main, medium_taps, taps, skip)


def states(gates, y_lo, y_hi, front, taps, poles):
    _, rows, channels = gates.shape
    ct = tile_of(channels, 512)
    lags = taps.shape[1]
    modes = poles.shape[0]
    line = lambda i: (0, i)
    cube = lambda i: (0, 0, i)
    return pl.pallas_call(
        functools.partial(states_kernel, step=64),
        grid=(channels // ct,),
        in_specs=[
            pl.BlockSpec((2, rows, ct), cube),
            pl.BlockSpec((rows // 2, ct), line),
            pl.BlockSpec((rows // 2, ct), line),
            pl.BlockSpec((3, rim, ct), cube),
            pl.BlockSpec((3, lags, ct), cube),
            pl.BlockSpec((modes, ct), line),
        ],
        out_specs=[
            pl.BlockSpec((rows, ct), line),
            pl.BlockSpec((rows, ct), line),
            pl.BlockSpec((modes, ct), line),
        ],
        out_shape=[
            jax.ShapeDtypeStruct((rows, channels), f32),
            jax.ShapeDtypeStruct((rows, channels), f32),
            jax.ShapeDtypeStruct((modes, channels), f32),
        ],
        scratch_shapes=[pltpu.VMEM((1, rows, ct), bf16)],
        compiler_params=params(),
        cost_estimate=cost(100 * rows * channels, 14 * rows * channels),
        name="states",
    )(gates, y_lo, y_hi, front, taps, poles)


def long_out(z_two, li_q, incoming, poles, residues, skip, piece, fan):
    rows, channels = z_two.shape
    modes = poles.shape[0]
    line = lambda i: (0, i)
    return pl.pallas_call(
        long_kernel,
        grid=(channels // piece,),
        in_specs=[
            pl.BlockSpec((rows, piece), line),
            pl.BlockSpec((rows, piece), line),
            pl.BlockSpec((modes, piece), line),
            pl.BlockSpec((modes, piece), line),
            pl.BlockSpec((modes, piece), line),
            pl.BlockSpec((1, piece), line),
        ],
        out_specs=pl.BlockSpec((1, rows, piece), lambda i: (i % fan, 0, i // fan)),
        out_shape=jax.ShapeDtypeStruct((fan, rows, channels // fan), bf16),
        compiler_params=params(),
        cost_estimate=cost(100 * rows * channels, 10 * rows * channels),
        name="long",
    )(z_two, li_q, incoming, poles, residues, skip)


def carried_state(state_end, poles, rows):
    count = lax.axis_size("seq")
    log_poles = jnp.log(poles)
    total = None
    for steps in range(1, min(inner, count - 1) + 1):
        term = from_behind(state_end, "seq", steps)
        if steps > 1:
            term = jnp.exp((rows * (steps - 1)) * log_poles) * term
        total = term if total is None else total + term
    window = inner
    while window < count:
        base = total
        for steps in range(window, min(window * inner, count), window):
            total = total + jnp.exp((rows * steps) * log_poles) * from_behind(base, "seq", steps)
        window *= inner
    return total


def dot(lhs, rhs):
    return jnp.dot(lhs, rhs, preferred_element_type=f32)


def swap(value, bit):
    count = lax.axis_size("seq")
    return lax.ppermute(value, "seq", [(source, source ^ bit) for source in range(count)])


def project_square(residual_in, y_fan, w_left, w_right):
    place = lax.rem(lax.axis_index("seq"), inner)
    parts = [lax.dynamic_index_in_dim(y_fan, place, 0, keepdims=False)]
    for bit in range(1, inner):
        outgoing = lax.dynamic_index_in_dim(y_fan, place ^ bit, 0, keepdims=False)
        parts.append(swap(outgoing, bit))
    mine = jnp.concatenate([parts[1], parts[3], parts[2], parts[0]], axis=0)
    other = lax.ppermute(mine, "tp", [(0, 1), (1, 0)])
    first = lax.axis_index("tp") == 0
    joined = jnp.concatenate(
        [jnp.where(first, mine, other), jnp.where(first, other, mine)], axis=1
    )
    rows = y_fan.shape[1]
    left_far = dot(joined[: 2 * rows], w_left).astype(bf16)
    right_far = dot(joined[rows : 3 * rows], w_right).astype(bf16)
    left_in = swap(left_far, 1)
    right_in = swap(right_far, 2)
    left_near = dot(joined[2 * rows :], w_left)
    right_one = dot(joined[:rows], w_right)
    right_own = dot(joined[3 * rows :], w_right)
    left_pass = (left_near[:rows] + left_in[rows:].astype(f32)).astype(bf16)
    right_pass = (right_one + right_in[:rows].astype(f32)).astype(bf16)
    left_last = swap(left_pass, 2)
    right_last = swap(right_pass, 1)
    left = left_near[rows:] + left_in[:rows].astype(f32) + left_last.astype(f32)
    right = right_own + right_in[rows:].astype(f32) + right_last.astype(f32)
    return (residual_in.astype(f32) + jnp.concatenate([left, right], axis=1)).astype(bf16)


def on_device(
    residual_in,
    features,
    short_mr,
    medium_taps,
    skip_mr,
    li_gates,
    short_li,
    poles,
    residues,
    skip_li,
    w_out,
):
    reach = medium_taps.shape[0]
    rows = features.shape[1]
    channels = features.shape[2]
    count = lax.axis_size("seq")
    blocks = channels // w_out.shape[0]
    square = lax.axis_size("tp") == 2 and count % inner == 0 and blocks % inner == 0
    if square:
        half = w_out.shape[1] // 2
        lines = [list(range(start, count, inner)) for start in range(inner)]
        gather = functools.partial(
            lax.all_gather, axis_name="seq", axis=0, tiled=True, axis_index_groups=lines
        )
        w_left = gather(w_out[:, :half])
        w_right = gather(w_out[:, half:])
    else:
        w_full = lax.all_gather(w_out, "seq", axis=0, tiled=True)
    tails = jnp.concatenate([features[:, rows - rim :], li_gates[:, rows - rim :]], axis=0)
    fronts = from_behind(tails, "seq", 1).astype(f32)
    mr_front = fronts[:3]
    skip_mr = skip_mr[None]
    z_one = gate(features, mr_front, short_mr)
    z_head = from_behind(z_one[rows - reach :], "seq", 1)
    q_mid = features[0, reach - rim : reach].astype(f32)
    y_hi = medium(features, 1, q_mid, z_one, z_one, 1, medium_taps, short_mr, skip_mr)
    y_front = from_behind(y_hi[reach - rim :], "seq", 1).astype(f32)
    y_lo = medium(features, 0, mr_front[0], z_head, z_one, 0, medium_taps, short_mr, skip_mr)
    li_front = jnp.concatenate([fronts[3:], y_front[None]], axis=0)
    li_q, z_two, state_end = states(li_gates, y_lo, y_hi, li_front, short_li, poles)
    incoming = carried_state(state_end, poles, rows)
    piece = w_out.shape[0]
    fan = inner if square else 1
    y_fan = long_out(z_two, li_q, incoming, poles, residues, skip_li[None], piece, fan)
    if square:
        return project_square(residual_in, y_fan, w_left, w_right)
    gathered = lax.all_gather(y_fan[0], "tp", axis=1, tiled=True)
    return (residual_in.astype(f32) + dot(gathered, w_full)).astype(bf16)


def solution(mesh):
    placed = (
        P("seq", "tp"),
        P(None, "seq", "tp"),
        P(None, None, "tp"),
        P(None, "tp"),
        P("tp"),
        P(None, "seq", "tp"),
        P(None, None, "tp"),
        P(None, "tp"),
        P(None, "tp"),
        P("tp"),
        P("seq", "tp"),
    )
    return jax.shard_map(
        on_device, mesh=mesh, in_specs=placed, out_specs=P("seq", "tp"), check_vma=False
    )
```

profile of v0, /device:TPU:0, one launch (start us, length us, event | category | flops | bytes accessed | tf_op | source)
XLA Modules:
  0.0 455.2 jit_solution(8465951840305627119)
XLA Ops:
  6.5 4.8 %fusion.20 = (bf16[512,2048]{1,0:T(8,128)(2,1)}, bf16[512,2048]{1,0:T(8,128)(2,1)}) fusion(bf16[512,4096]{1,0:T(8,128)(2,1)} %param.21), kind=kLoop, calls=%fused_computation.46 | loop fusion | bytes 8388608 | tf_op jit(solution)/shard_map/slice | solution.py:331
  12.4 4.9 %collective-permute-start = (bf16[5,8,4096]{2,1,0:T(8,128)(2,1)S(1)}, bf16[5,8,4096]{2,1,0:T(8,128)(2,1)S(1)}, u32[]{:S(2)}, u32[]{:S(2)}) collective-permute-start(bf16[5,8,4096]{2,1,0:T(8,128)(2,1)S(1)} %pad_maximum_fusion.4), channel_id=1, source_target_pairs={{0,2},{2,4},{4,6},{6,8},{8,10},{10,12},{12,14},{14,16},{16,18},{18... | collective-permute-start | bytes 983048 | tf_op jit(solution)/shard_map/ppermute | solution.py:17
  18.1 6.1 %collective-permute-done = bf16[5,8,4096]{2,1,0:T(8,128)(2,1)S(1)} collective-permute-done((bf16[5,8,4096]{2,1,0:T(8,128)(2,1)S(1)}, bf16[5,8,4096]{2,1,0:T(8,128)(2,1)S(1)}, u32[]{:S(2)}, u32[]{:S(2)}) %collective-permute-start) | collective-permute-done | bytes 327712 | tf_op jit(solution)/shard_map/ppermute | solution.py:17
  24.2 12.5 %gate.1.main_ref.head_ref = bf16[256,4096]{1,0:T(8,128)(2,1)S(1)} custom-call(bf16[3,256,4096]{2,1,0:T(8,128)(2,1)} %q_ref.3, bf16[3,256,4096]{2,1,0:T(8,128)(2,1)} %q_ref.3, f32[3,8,4096]{2,1,0:T(8,128)S(1)} %slice.86.front_ref, f32[3,7,4096]{2,1,0:T(8,128)S(1)} %copy-done.1), custom_call_target="tpu_custom_call" | custom-call | flops 62914560 | bytes 6291456 | tf_op jit(solution)/shard_map/gate/pallas_call | solution.py:148
  36.8 4.4 collective-permute-start.1
  41.3 26.8 %medium.3.yhi_ref = bf16[128,4096]{1,0:T(8,128)(2,1)S(1)} custom-call(bf16[3,256,4096]{2,1,0:T(8,128)(2,1)} %q_ref.3, f32[8,4096]{1,0:T(8,128)S(1)} %bitcast_convert_fusion.1.front_ref, bf16[256,4096]{1,0:T(8,128)(2,1)S(1)} %gate.1.main_ref.head_ref, bf16[256,4096]{1,0:T(8,128)(2,1)S(1)} %gate.1.main_ref.head_ref, bf16[128,256]{1,0:T(8,128)(2,1)S(1)} %copy-done.3, ...), custom_call_target="tpu_custom_call" | custom-call | flops 1310720000 | bytes 4194304 | tf_op jit(solution)/shard_map/medium/pallas_call | solution.py:171
  68.1 4.2 collective-permute-start.2
  74.3 26.9 %medium.2.ylo_ref = bf16[128,4096]{1,0:T(8,128)(2,1)S(1)} custom-call(bf16[3,256,4096]{2,1,0:T(8,128)(2,1)} %q_ref.3, f32[8,4096]{1,0:T(8,128)S(1)} %slice_bitcast_fusion.front_ref, bf16[128,4096]{1,0:T(8,128)(2,1)S(1)} %collective-permute-done.1.head_ref, bf16[256,4096]{1,0:T(8,128)(2,1)S(1)} %gate.1.main_ref.head_ref, bf16[128,256]{1,0:T(8,128)(2,1)S(1)} %copy-done.3, ...), custom_call_target="tpu_custom_call" | custom-call | flops 1310720000 | bytes 4194304 | tf_op jit(solution)/shard_map/medium/pallas_call | solution.py:171
  101.2 19.5 %states.1 = (f32[256,4096]{1,0:T(8,128)}, f32[256,4096]{1,0:T(8,128)}, f32[16,4096]{1,0:T(8,128)S(1)}) custom-call(bf16[2,256,4096]{2,1,0:T(8,128)(2,1)} %g_ref.1, bf16[128,4096]{1,0:T(8,128)(2,1)S(1)} %medium.2.ylo_ref, bf16[128,4096]{1,0:T(8,128)(2,1)S(1)} %medium.3.yhi_ref, f32[3,8,4096]{2,1,0:T(8,128)S(1)} %pad_maximum_fusion.3.front_ref, ...), custom_call_target="tpu_custom_call" | custom-call | flops 104857600 | bytes 14680064 | tf_op jit(solution)/shard_map/states/pallas_call | solution.py:199
  120.7 4.4 collective-permute-start.3
  125.1 19.5 %collective-permute-start.4 = (f32[16,4096]{1,0:T(8,128)S(1)}, f32[16,4096]{1,0:T(8,128)S(1)}, u32[]{:S(2)}, u32[]{:S(2)}) collective-permute-start(f32[16,4096]{1,0:T(8,128)S(1)} %get-tuple-element.10), channel_id=1, source_target_pairs={{0,4},{2,6},{4,8},{6,10},{8,12},{10,14},{12,16},{14,18},{16,20},{1... | collective-permute-start | bytes 786440 | tf_op jit(solution)/shard_map/ppermute | solution.py:17
  144.5 5.6 %collective-permute-start.5 = (f32[16,4096]{1,0:T(8,128)S(1)}, f32[16,4096]{1,0:T(8,128)S(1)}, u32[]{:S(2)}, u32[]{:S(2)}) collective-permute-start(f32[16,4096]{1,0:T(8,128)S(1)} %get-tuple-element.10), channel_id=1, source_target_pairs={{0,6},{2,8},{4,10},{6,12},{8,14},{10,16},{12,18},{14,20},{16,22},{... | collective-permute-start | bytes 786440 | tf_op jit(solution)/shard_map/ppermute | solution.py:17
  150.2 25.9 %collective-permute-start.6 = (f32[16,4096]{1,0:T(8,128)S(1)}, f32[16,4096]{1,0:T(8,128)S(1)}, u32[]{:S(2)}, u32[]{:S(2)}) collective-permute-start(f32[16,4096]{1,0:T(8,128)S(1)} %get-tuple-element.10), channel_id=1, source_target_pairs={{0,8},{2,10},{4,12},{6,14},{8,16},{10,18},{12,20},{14,22},{16,24},... | collective-permute-start | bytes 786440 | tf_op jit(solution)/shard_map/ppermute | solution.py:17
  176.2 3.8 collective-permute-done.6
  180.2 8.3 %collective-permute-start.7 = (f32[16,4096]{1,0:T(8,128)S(1)}, f32[16,4096]{1,0:T(8,128)S(1)}, u32[]{:S(2)}, u32[]{:S(2)}) collective-permute-start(f32[16,4096]{1,0:T(8,128)S(1)} %multiply_add_fusion.1), channel_id=1, source_target_pairs={{0,8},{2,10},{4,12},{6,14},{8,16},{10,18},{12,20},{14,22},{16,24},... | collective-permute-start | bytes 786440 | tf_op jit(solution)/shard_map/ppermute | solution.py:17
  188.5 8.1 %collective-permute-start.8 = (f32[16,4096]{1,0:T(8,128)S(1)}, f32[16,4096]{1,0:T(8,128)S(1)}, u32[]{:S(2)}, u32[]{:S(2)}) collective-permute-start(f32[16,4096]{1,0:T(8,128)S(1)} %multiply_add_fusion.1), channel_id=1, source_target_pairs={{0,16},{2,18},{4,20},{6,22},{8,24},{10,26},{12,28},{14,30},{1,17},... | collective-permute-start | bytes 786440 | tf_op jit(solution)/shard_map/ppermute | solution.py:17
  198.1 5.2 %collective-permute-done.8 = f32[16,4096]{1,0:T(8,128)S(1)} collective-permute-done((f32[16,4096]{1,0:T(8,128)S(1)}, f32[16,4096]{1,0:T(8,128)S(1)}, u32[]{:S(2)}, u32[]{:S(2)}) %collective-permute-start.8) | collective-permute-done | bytes 262176 | tf_op jit(solution)/shard_map/ppermute | solution.py:17
  203.3 3.5 collective-permute-done.9
  207.0 18.4 %long.1 = bf16[4,256,1024]{2,1,0:T(8,128)(2,1)S(1)} custom-call(f32[256,4096]{1,0:T(8,128)} %get-tuple-element.8.z_ref, f32[256,4096]{1,0:T(8,128)} %get-tuple-element.9.q_ref, f32[16,4096]{1,0:T(8,128)S(1)} %multiply_add_fusion.in_ref, f32[16,4096]{1,0:T(8,128)S(1)} %copy-done, f32[16,4096]{1,0:T(8,128)S(1)} %copy-done.4, f32[1,4096]{1,0:T(1,128)S(1)} %bitcast.25), custom_call_target="tpu_custom_call" | custom-call | flops 104857600 | bytes 10485760 | tf_op jit(solution)/shard_map/long/pallas_call | solution.py:231
  225.6 10.1 %collective-permute-start.10 = (bf16[256,1024]{1,0:T(8,128)(2,1)S(1)}, bf16[256,1024]{1,0:T(8,128)(2,1)S(1)}, u32[]{:S(2)}, u32[]{:S(2)}) collective-permute-start(bf16[256,1024]{1,0:T(8,128)(2,1)S(1)} %get-tuple-element.15), channel_id=1, source_target_pairs={{0,2},{2,0},{4,6},{6,4},{8,10},{10,8},{12,14},{14,12},{16,18},{18,... | collective-permute-start | bytes 1572872 | tf_op jit(solution)/shard_map/ppermute | solution.py:274
  235.6 20.2 %collective-permute-start.11 = (bf16[256,1024]{1,0:T(8,128)(2,1)S(1)}, bf16[256,1024]{1,0:T(8,128)(2,1)S(1)}, u32[]{:S(2)}, u32[]{:S(2)}) collective-permute-start(bf16[256,1024]{1,0:T(8,128)(2,1)S(1)} %get-tuple-element.18), channel_id=1, source_target_pairs={{0,6},{2,4},{4,2},{6,0},{8,14},{10,12},{12,10},{14,8},{16,22},{18,... | collective-permute-start | bytes 1572872 | tf_op jit(solution)/shard_map/ppermute | solution.py:274
  256.4 20.0 %collective-permute-done.11 = bf16[256,1024]{1,0:T(8,128)(2,1)S(1)} collective-permute-done((bf16[256,1024]{1,0:T(8,128)(2,1)S(1)}, bf16[256,1024]{1,0:T(8,128)(2,1)S(1)}, u32[]{:S(2)}, u32[]{:S(2)}) %collective-permute-start.11) | collective-permute-done | bytes 524320 | tf_op jit(solution)/shard_map/ppermute | solution.py:274
  278.6 4.3 collective-permute-done.13
  282.9 3.4 broadcast_select_fusion
  286.3 9.5 %convolution_convert_fusion.1 = bf16[512,2048]{1,0:T(8,128)(2,1)} fusion(bf16[2048,2048]{1,0:T(8,128)(2,1)} %all-gather.3.cloned.1.call-done, bf16[1024,1024]{1,0:T(8,128)(2,1)} %get-tuple-element.14, bf16[1024,1024]{1,0:T(8,128)(2,1)S(1)} %get-tuple-element.13), kind=kOutput, calls=%fused_computation.11 | convolution fusion | flops 4300210176 | bytes 14680064 | tf_op jit(solution)/shard_map/dot_general | solution.py:269
  297.5 60.1 %all-gather.5.cloned.1.call-done = bf16[2048,2048]{1,0:T(8,128)(2,1)} async-done(((bf16[512,2048]{1,0:T(8,128)(2,1)}), bf16[2048,2048]{1,0:T(8,128)(2,1)}) %all-gather.5.cloned.1.call-update) | async-done | bytes 8388624 | tf_op jit(solution)/shard_map/all_gather | solution.py:332
  357.6 8.3 %convolution_convert_fusion = bf16[512,2048]{1,0:T(8,128)(2,1)S(1)} fusion(bf16[2048,2048]{1,0:T(8,128)(2,1)} %all-gather.5.cloned.1.call-done, bf16[1024,1024]{1,0:T(8,128)(2,1)} %get-tuple-element.14, bf16[1024,1024]{1,0:T(8,128)(2,1)S(1)} %get-tuple-element.13), kind=kOutput, calls=%fused_computation.10 | convolution fusion | flops 4300210176 | bytes 14680064 | tf_op jit(solution)/shard_map/dot_general | solution.py:269
  367.5 7.1 %fusion.6 = f32[512,2048]{1,0:T(8,128)S(1)} fusion(bf16[2048,2048]{1,0:T(8,128)(2,1)} %all-gather.3.cloned.1.call-done, bf16[1024,1024]{1,0:T(8,128)(2,1)S(1)} %copy-done.8, bf16[1024,1024]{1,0:T(8,128)(2,1)S(1)} %get-tuple-element.13), kind=kOutput, calls=%fused_computation.18 | convolution fusion | flops 4299161600 | bytes 16777216 | tf_op jit(solution)/shard_map/dot_general | solution.py:269
  377.1 37.4 %collective-permute-done.16 = bf16[512,2048]{1,0:T(8,128)(2,1)S(1)} collective-permute-done((bf16[512,2048]{1,0:T(8,128)(2,1)S(1)}, bf16[512,2048]{1,0:T(8,128)(2,1)S(1)}, u32[]{:S(2)}, u32[]{:S(2)}) %collective-permute-start.16) | collective-permute-done | bytes 2097184 | tf_op jit(solution)/shard_map/ppermute | solution.py:274
  416.9 4.7 %collective-permute-start.17 = (bf16[256,2048]{1,0:T(8,128)(2,1)S(1)}, bf16[256,2048]{1,0:T(8,128)(2,1)S(1)}, u32[]{:S(2)}, u32[]{:S(2)}) collective-permute-start(bf16[256,2048]{1,0:T(8,128)(2,1)S(1)} %fusion.2), channel_id=1, source_target_pairs={{0,2},{2,0},{4,6},{6,4},{8,10},{10,8},{12,14},{14,12},{16,18},{18,... | collective-permute-start | bytes 3145736 | tf_op jit(solution)/shard_map/ppermute | solution.py:274
  421.6 14.5 %collective-permute-done.15 = bf16[256,2048]{1,0:T(8,128)(2,1)S(1)} collective-permute-done((bf16[256,2048]{1,0:T(8,128)(2,1)S(1)}, bf16[256,2048]{1,0:T(8,128)(2,1)S(1)}, u32[]{:S(2)}, u32[]{:S(2)}) %collective-permute-start.15) | collective-permute-done | bytes 1048608 | tf_op jit(solution)/shard_map/ppermute | solution.py:274
  437.8 6.1 %collective-permute-done.17 = bf16[256,2048]{1,0:T(8,128)(2,1)S(1)} collective-permute-done((bf16[256,2048]{1,0:T(8,128)(2,1)S(1)}, bf16[256,2048]{1,0:T(8,128)(2,1)S(1)}, u32[]{:S(2)}, u32[]{:S(2)}) %collective-permute-start.17) | collective-permute-done | bytes 1048608 | tf_op jit(solution)/shard_map/ppermute | solution.py:274
  (70 shorter events, 22.8 us)
Async XLA Ops:
  6.5 279.8 %all-gather.3.cloned.1.call-start = ((), (), s32[]{:S(2)}) async-start(), calls=%async_computation | async-start | bytes 10485760 | tf_op jit(solution)/shard_map/all_gather | solution.py:331
  11.4 346.2 %all-gather.5.cloned.1.call-start = ((), (), s32[]{:S(2)}) async-start(), calls=%async_computation.1 | async-start | bytes 10485760 | tf_op jit(solution)/shard_map/all_gather | solution.py:332
  11.4 12.8 %copy-start.1 = (f32[3,7,4096]{2,1,0:T(8,128)S(1)}, f32[3,7,4096]{2,1,0:T(8,128)}, u32[]{:S(2)}) copy-start(f32[3,7,4096]{2,1,0:T(8,128)} %taps_ref.6) | copy-start | bytes 1032196
  12.4 11.8 %collective-permute-start = (bf16[5,8,4096]{2,1,0:T(8,128)(2,1)S(1)}, bf16[5,8,4096]{2,1,0:T(8,128)(2,1)S(1)}, u32[]{:S(2)}, u32[]{:S(2)}) collective-permute-start(bf16[5,8,4096]{2,1,0:T(8,128)(2,1)S(1)} %pad_maximum_fusion.4), channel_id=1, source_target_pairs={{0,2},{2,4},{4,6},{6,8},{8,10},{10,12},{12,14},{14,16},{16,18},{18... | collective-permute-start | bytes 983048 | tf_op jit(solution)/shard_map/ppermute | solution.py:17
  36.7 4.6 %copy-start.3 = (bf16[128,256]{1,0:T(8,128)(2,1)S(1)}, bf16[128,256]{1,0:T(8,128)(2,1)}, u32[]{:S(2)}) copy-start(bf16[128,256]{1,0:T(8,128)(2,1)} %med_ref.3) | copy-start | bytes 196612
  36.7 4.6 %copy-start.5 = (f32[4096]{0:T(1024)S(1)}, f32[4096]{0:T(1024)}, u32[]{:S(2)}) copy-start(f32[4096]{0:T(1024)} %param.15) | copy-start | bytes 49156
  36.8 37.4 %collective-permute-start.1 = (bf16[128,4096]{1,0:T(8,128)(2,1)S(1)}, bf16[128,4096]{1,0:T(8,128)(2,1)S(1)}, u32[]{:S(2)}, u32[]{:S(2)}) collective-permute-start(bf16[128,4096]{1,0:T(8,128)(2,1)S(1)} %slice.87), channel_id=1, source_target_pairs={{0,2},{2,4},{4,6},{6,8},{8,10},{10,12},{12,14},{14,16},{16,18},{18... | collective-permute-start | bytes 3145736 | tf_op jit(solution)/shard_map/ppermute | solution.py:17
  68.1 6.1 %collective-permute-start.2 = (bf16[8,4096]{1,0:T(8,128)(2,1)S(1)}, bf16[8,4096]{1,0:T(8,128)(2,1)S(1)}, u32[]{:S(2)}, u32[]{:S(2)}) collective-permute-start(bf16[8,4096]{1,0:T(8,128)(2,1)S(1)} %slice.89), channel_id=1, source_target_pairs={{0,2},{2,4},{4,6},{6,8},{8,10},{10,12},{12,14},{14,16},{16,18},{18... | collective-permute-start | bytes 196616 | tf_op jit(solution)/shard_map/ppermute | solution.py:17
  74.3 26.9 %copy-start = (f32[16,4096]{1,0:T(8,128)S(1)}, f32[16,4096]{1,0:T(8,128)}, u32[]{:S(2)}) copy-start(f32[16,4096]{1,0:T(8,128)} %poles_ref.3) | copy-start | bytes 786436
  74.3 26.9 %copy-start.2 = (f32[3,7,4096]{2,1,0:T(8,128)S(1)}, f32[3,7,4096]{2,1,0:T(8,128)}, u32[]{:S(2)}) copy-start(f32[3,7,4096]{2,1,0:T(8,128)} %taps_ref.7) | copy-start | bytes 1032196
  120.7 86.3 %copy-start.4 = (f32[16,4096]{1,0:T(8,128)S(1)}, f32[16,4096]{1,0:T(8,128)}, u32[]{:S(2)}) copy-start(f32[16,4096]{1,0:T(8,128)} %res_ref.1) | copy-start | bytes 786436
  120.7 86.3 %copy-start.6 = (f32[4096]{0:T(1024)S(1)}, f32[4096]{0:T(1024)}, u32[]{:S(2)}) copy-start(f32[4096]{0:T(1024)} %param.20) | copy-start | bytes 49156
  120.7 55.5 %collective-permute-start.3 = (f32[16,4096]{1,0:T(8,128)S(1)}, f32[16,4096]{1,0:T(8,128)S(1)}, u32[]{:S(2)}, u32[]{:S(2)}) collective-permute-start(f32[16,4096]{1,0:T(8,128)S(1)} %get-tuple-element.10), channel_id=1, source_target_pairs={{0,2},{2,4},{4,6},{6,8},{8,10},{10,12},{12,14},{14,16},{16,18},{18... | collective-permute-start | bytes 786440 | tf_op jit(solution)/shard_map/ppermute | solution.py:17
  125.1 51.1 %collective-permute-start.4 = (f32[16,4096]{1,0:T(8,128)S(1)}, f32[16,4096]{1,0:T(8,128)S(1)}, u32[]{:S(2)}, u32[]{:S(2)}) collective-permute-start(f32[16,4096]{1,0:T(8,128)S(1)} %get-tuple-element.10), channel_id=1, source_target_pairs={{0,4},{2,6},{4,8},{6,10},{8,12},{10,14},{12,16},{14,18},{16,20},{1... | collective-permute-start | bytes 786440 | tf_op jit(solution)/shard_map/ppermute | solution.py:17
  144.5 31.6 %collective-permute-start.5 = (f32[16,4096]{1,0:T(8,128)S(1)}, f32[16,4096]{1,0:T(8,128)S(1)}, u32[]{:S(2)}, u32[]{:S(2)}) collective-permute-start(f32[16,4096]{1,0:T(8,128)S(1)} %get-tuple-element.10), channel_id=1, source_target_pairs={{0,6},{2,8},{4,10},{6,12},{8,14},{10,16},{12,18},{14,20},{16,22},{... | collective-permute-start | bytes 786440 | tf_op jit(solution)/shard_map/ppermute | solution.py:17
  150.2 29.8 %collective-permute-start.6 = (f32[16,4096]{1,0:T(8,128)S(1)}, f32[16,4096]{1,0:T(8,128)S(1)}, u32[]{:S(2)}, u32[]{:S(2)}) collective-permute-start(f32[16,4096]{1,0:T(8,128)S(1)} %get-tuple-element.10), channel_id=1, source_target_pairs={{0,8},{2,10},{4,12},{6,14},{8,16},{10,18},{12,20},{14,22},{16,24},... | collective-permute-start | bytes 786440 | tf_op jit(solution)/shard_map/ppermute | solution.py:17
  180.2 17.9 %collective-permute-start.7 = (f32[16,4096]{1,0:T(8,128)S(1)}, f32[16,4096]{1,0:T(8,128)S(1)}, u32[]{:S(2)}, u32[]{:S(2)}) collective-permute-start(f32[16,4096]{1,0:T(8,128)S(1)} %multiply_add_fusion.1), channel_id=1, source_target_pairs={{0,8},{2,10},{4,12},{6,14},{8,16},{10,18},{12,20},{14,22},{16,24},... | collective-permute-start | bytes 786440 | tf_op jit(solution)/shard_map/ppermute | solution.py:17
  188.5 14.8 %collective-permute-start.8 = (f32[16,4096]{1,0:T(8,128)S(1)}, f32[16,4096]{1,0:T(8,128)S(1)}, u32[]{:S(2)}, u32[]{:S(2)}) collective-permute-start(f32[16,4096]{1,0:T(8,128)S(1)} %multiply_add_fusion.1), channel_id=1, source_target_pairs={{0,16},{2,18},{4,20},{6,22},{8,24},{10,26},{12,28},{14,30},{1,17},... | collective-permute-start | bytes 786440 | tf_op jit(solution)/shard_map/ppermute | solution.py:17
  196.5 10.2 %collective-permute-start.9 = (f32[16,4096]{1,0:T(8,128)S(1)}, f32[16,4096]{1,0:T(8,128)S(1)}, u32[]{:S(2)}, u32[]{:S(2)}) collective-permute-start(f32[16,4096]{1,0:T(8,128)S(1)} %multiply_add_fusion.1), channel_id=1, source_target_pairs={{0,24},{2,26},{4,28},{6,30},{1,25},{3,27},{5,29},{7,31}} | collective-permute-start | bytes 786440 | tf_op jit(solution)/shard_map/ppermute | solution.py:17
  225.6 30.8 %collective-permute-start.10 = (bf16[256,1024]{1,0:T(8,128)(2,1)S(1)}, bf16[256,1024]{1,0:T(8,128)(2,1)S(1)}, u32[]{:S(2)}, u32[]{:S(2)}) collective-permute-start(bf16[256,1024]{1,0:T(8,128)(2,1)S(1)} %get-tuple-element.15), channel_id=1, source_target_pairs={{0,2},{2,0},{4,6},{6,4},{8,10},{10,8},{12,14},{14,12},{16,18},{18,... | collective-permute-start | bytes 1572872 | tf_op jit(solution)/shard_map/ppermute | solution.py:274
  235.6 40.7 %collective-permute-start.11 = (bf16[256,1024]{1,0:T(8,128)(2,1)S(1)}, bf16[256,1024]{1,0:T(8,128)(2,1)S(1)}, u32[]{:S(2)}, u32[]{:S(2)}) collective-permute-start(bf16[256,1024]{1,0:T(8,128)(2,1)S(1)} %get-tuple-element.18), channel_id=1, source_target_pairs={{0,6},{2,4},{4,2},{6,0},{8,14},{10,12},{12,10},{14,8},{16,22},{18,... | collective-permute-start | bytes 1572872 | tf_op jit(solution)/shard_map/ppermute | solution.py:274
  255.9 21.9 %collective-permute-start.12 = (bf16[256,1024]{1,0:T(8,128)(2,1)S(1)}, bf16[256,1024]{1,0:T(8,128)(2,1)S(1)}, u32[]{:S(2)}, u32[]{:S(2)}) collective-permute-start(bf16[256,1024]{1,0:T(8,128)(2,1)S(1)} %get-tuple-element.17), channel_id=1, source_target_pairs={{0,4},{2,6},{4,0},{6,2},{8,12},{10,14},{12,8},{14,10},{16,20},{18,... | collective-permute-start | bytes 1572872 | tf_op jit(solution)/shard_map/ppermute | solution.py:274
  276.3 1.6 copy-start.9
  278.6 4.3 collective-permute-start.13
  295.8 78.9 %collective-permute-start.14 = (bf16[512,2048]{1,0:T(8,128)(2,1)}, bf16[512,2048]{1,0:T(8,128)(2,1)}, u32[]{:S(2)}, u32[]{:S(2)}) collective-permute-start(bf16[512,2048]{1,0:T(8,128)(2,1)} %convolution_convert_fusion.1), channel_id=1, source_target_pairs={{0,2},{2,0},{4,6},{6,4},{8,10},{10,8},{12,14},{14,12},{16,18},{18,... | collective-permute-start | bytes 6291464 | tf_op jit(solution)/shard_map/ppermute | solution.py:274
  357.6 9.9 %copy-start.8 = (bf16[1024,1024]{1,0:T(8,128)(2,1)S(1)}, bf16[1024,1024]{1,0:T(8,128)(2,1)}, u32[]{:S(2)}) copy-start(bf16[1024,1024]{1,0:T(8,128)(2,1)} %get-tuple-element.14) | copy-start | bytes 6291460
  357.6 56.9 %slice-start.2 = ((s8[8388608]{0:T(1024)(128)(4,1)}), s8[4194304]{0:T(1024)(128)(4,1)S(1)}, s32[]{:S(2)}) async-start(s8[8388608]{0:T(1024)(128)(4,1)} %bitcast.26), calls=%async_computation.4 | async-start | bytes 8388608
  366.0 48.6 %slice-start.3 = ((s8[8388608]{0:T(1024)(128)(4,1)}), s8[4194304]{0:T(1024)(128)(4,1)S(1)}, s32[]{:S(2)}) async-start(s8[8388608]{0:T(1024)(128)(4,1)} %bitcast.26), calls=%async_computation.5 | async-start | bytes 8388608
  366.0 48.5 %collective-permute-start.16 = (bf16[512,2048]{1,0:T(8,128)(2,1)S(1)}, bf16[512,2048]{1,0:T(8,128)(2,1)S(1)}, u32[]{:S(2)}, u32[]{:S(2)}) collective-permute-start(bf16[512,2048]{1,0:T(8,128)(2,1)S(1)} %convolution_convert_fusion), channel_id=1, source_target_pairs={{0,4},{2,6},{4,0},{6,2},{8,12},{10,14},{12,8},{14,10},{16,20},{18,... | collective-permute-start | bytes 6291464 | tf_op jit(solution)/shard_map/ppermute | solution.py:274
  376.3 59.8 %collective-permute-start.15 = (bf16[256,2048]{1,0:T(8,128)(2,1)S(1)}, bf16[256,2048]{1,0:T(8,128)(2,1)S(1)}, u32[]{:S(2)}, u32[]{:S(2)}) collective-permute-start(bf16[256,2048]{1,0:T(8,128)(2,1)S(1)} %fusion.10), channel_id=1, source_target_pairs={{0,4},{2,6},{4,0},{6,2},{8,12},{10,14},{12,8},{14,10},{16,20},{18,... | collective-permute-start | bytes 3145736 | tf_op jit(solution)/shard_map/ppermute | solution.py:274
  416.9 27.0 %collective-permute-start.17 = (bf16[256,2048]{1,0:T(8,128)(2,1)S(1)}, bf16[256,2048]{1,0:T(8,128)(2,1)S(1)}, u32[]{:S(2)}, u32[]{:S(2)}) collective-permute-start(bf16[256,2048]{1,0:T(8,128)(2,1)S(1)} %fusion.2), channel_id=1, source_target_pairs={{0,2},{2,0},{4,6},{6,4},{8,10},{10,8},{12,14},{14,12},{16,18},{18,... | collective-permute-start | bytes 3145736 | tf_op jit(solution)/shard_map/ppermute | solution.py:274
  437.8 8.7 %copy-start.7 = (bf16[256,4096]{1,0:T(8,128)(2,1)S(1)}, bf16[256,4096]{1,0:T(8,128)(2,1)}, u32[]{:S(2)}) copy-start(bf16[256,4096]{1,0:T(8,128)(2,1)} %param.11) | copy-start | bytes 6291460
  (3 other events, 2.7 us)
Sparse Core Ops, SparseCore 0:
  11.5 152.3 all-gather.2
  165.4 192.1 all-gather.4
where the time goes:
time: 462 us; the launch traced here: 455 us
  waiting for transfers between devices  165 us (36%)
  starting transfers between devices  126 us (27%)
  Pallas kernels  104 us (23%)
  matrix products  29.9 us (6%)
  between operations  13.9 us (3%)
  other arithmetic  10 us (2%)
  local copies, waits for them, and re-layouts  6.05 us (1%)
    ppermute x10, starting transfers between devices, from_behind(): lax.ppermute(value, axis, [(source, source + steps) for source in range(c...  86.8 us
    ppermute x7, waiting for transfers between devices, swap(): lax.ppermute(value, 'seq', [(source, source ^ bit) for source in range(co...  79.4 us
    all_gather x1, waiting for transfers between devices, on_device(): w_right = gather(w_out[:, half:])  60.1 us
    pallas_call x2, Pallas kernels, medium(): pl.pallas_call(functools.partial(medium_kernel, width=channels // groups)...  53.6 us
    ppermute x7, starting transfers between devices, swap(): lax.ppermute(value, 'seq', [(source, source ^ bit) for source in range(co...  39.6 us
    dot_general x5, matrix products, dot(): return jnp.dot(lhs, rhs, preferred_element_type=f32)  29.9 us
    ppermute x10, waiting for transfers between devices, from_behind(): lax.ppermute(value, axis, [(source, source + steps) for source in range(c...  20.4 us
    pallas_call x1, Pallas kernels, states(): pl.pallas_call(functools.partial(states_kernel, step=64), grid=(channels...  19.5 us
  transfers between devices with their start and end apart: 20, of which 12 were waited for; matrix products, arithmetic and copies ran while one was open for 8% of the time, Pallas kernels for 23%

commit v1 on v0

--- a/solution.py
+++ b/solution.py
@@ -274,7 +274,62 @@
     return lax.ppermute(value, "seq", [(source, source ^ bit) for source in range(count)])
 
 
-def project_square(residual_in, y_fan, w_left, w_right):
+def square_state(state_end, poles, rows):
+    count = lax.axis_size("seq")
+    log_poles = jnp.log(poles)
+    place = lax.rem(lax.axis_index("seq"), inner)
+    inside = jnp.zeros_like(state_end)
+    whole = jnp.zeros_like(state_end)
+    for bit in range(inner):
+        state = state_end if bit == 0 else swap(state_end, bit)
+        source = place ^ bit
+        lag = (rows * (inner - 1 - source)).astype(f32)
+        whole = whole + jnp.exp(lag * log_poles) * state
+        if bit > 0:
+            ahead = place - 1 - source
+            lag = (rows * jnp.maximum(ahead, 0)).astype(f32)
+            inside = inside + jnp.where(ahead >= 0, jnp.exp(lag * log_poles) * state, 0.0)
+    before = None
+    for steps in range(1, count // inner):
+        term = from_behind(whole, "seq", steps * inner)
+        if steps > 1:
+            term = jnp.exp((rows * inner * (steps - 1)) * log_poles) * term
+        before = term if before is None else before + term
+    if before is None:
+        return inside
+    return inside + jnp.exp((rows * place).astype(f32) * log_poles) * before
+
+
+def product_kernel(x_ref, w_ref, *rest):
+    out_ref = rest[-1]
+    out_ref[...] = jnp.dot(
+        x_ref[...], w_ref[...], preferred_element_type=f32
+    ).astype(out_ref.dtype)
+
+
+def product(x, w, block, first_row, row_blocks, first_column, columns, kind, after=()):
+    depth = x.shape[1]
+    ct = tile_of(columns, 512)
+    base = first_column // ct
+    return pl.pallas_call(
+        product_kernel,
+        grid=(columns // ct, row_blocks),
+        in_specs=[
+            pl.BlockSpec((block, depth), lambda j, i: (first_row + i, 0)),
+            pl.BlockSpec((depth, ct), lambda j, i: (0, base + j)),
+        ]
+        + [pl.BlockSpec(memory_space=pl.ANY)] * len(after),
+        out_specs=pl.BlockSpec((block, ct), lambda j, i: (i, j)),
+        out_shape=jax.ShapeDtypeStruct((block * row_blocks, columns), kind),
+        compiler_params=pltpu.CompilerParams(vmem_limit_bytes=40 * 1024 * 1024),
+        cost_estimate=cost(
+            2 * block * row_blocks * depth * columns, 2 * depth * columns
+        ),
+        name="product",
+    )(x, w, *after)
+
+
+def project_square(residual_in, y_fan, w_wide, w_last):
     place = lax.rem(lax.axis_index("seq"), inner)
     parts = [lax.dynamic_index_in_dim(y_fan, place, 0, keepdims=False)]
     for bit in range(1, inner):
@@ -287,20 +342,40 @@
         [jnp.where(first, mine, other), jnp.where(first, other, mine)], axis=1
     )
     rows = y_fan.shape[1]
-    left_far = dot(joined[: 2 * rows], w_left).astype(bf16)
-    right_far = dot(joined[rows : 3 * rows], w_right).astype(bf16)
-    left_in = swap(left_far, 1)
-    right_in = swap(right_far, 2)
-    left_near = dot(joined[2 * rows :], w_left)
-    right_one = dot(joined[:rows], w_right)
-    right_own = dot(joined[3 * rows :], w_right)
-    left_pass = (left_near[:rows] + left_in[rows:].astype(f32)).astype(bf16)
-    right_pass = (right_one + right_in[:rows].astype(f32)).astype(bf16)
-    left_last = swap(left_pass, 2)
-    right_last = swap(right_pass, 1)
-    left = left_near[rows:] + left_in[:rows].astype(f32) + left_last.astype(f32)
-    right = right_own + right_in[rows:].astype(f32) + right_last.astype(f32)
-    return (residual_in.astype(f32) + jnp.concatenate([left, right], axis=1)).astype(bf16)
+
+    def left_sums(far, pass_on, own):
+        arrived = swap(far, 1).astype(f32)
+        return (pass_on + arrived[rows:]).astype(bf16), own + arrived[:rows]
+
+    def right_sums(far, pass_on, own):
+        arrived = swap(far, 2).astype(f32)
+        return (pass_on + arrived[:rows]).astype(bf16), own + arrived[rows:]
+
+    wide = w_wide.shape[1] // 2
+    far_left = product(joined, w_wide, rows, 0, 2, 0, wide, bf16)
+    far_right = product(joined, w_wide, rows, 1, 2, wide, wide, bf16)
+    near_left = product(joined, w_wide, rows, 2, 2, 0, wide, f32)
+    near_right = product(joined, w_wide, rows, 0, 1, wide, wide, f32)
+    own_right = product(joined, w_wide, rows, 3, 1, wide, wide, f32)
+    left_pass, left_own = left_sums(far_left, near_left[:rows], near_left[rows:])
+    right_pass, right_own = right_sums(far_right, near_right, own_right)
+    left_end = swap(left_pass, 2)
+    right_end = swap(right_pass, 1)
+    left = left_own + left_end.astype(f32)
+    right = right_own + right_end.astype(f32)
+    half = w_last.shape[1] // 2
+    ends = (left_end, right_end)
+    far_l = product(joined, w_last, rows, 0, 2, 0, half, bf16, ends)
+    far_r = product(joined, w_last, rows, 1, 2, half, half, bf16, ends)
+    near_l = product(joined, w_last, rows, 2, 2, 0, half, f32)
+    near_r = product(joined, w_last, rows, 0, 1, half, half, f32)
+    last_r = product(joined, w_last, rows, 3, 1, half, half, f32)
+    pass_l, own_l = left_sums(far_l, near_l[:rows], near_l[rows:])
+    pass_r, own_r = right_sums(far_r, near_r, last_r)
+    end_l = own_l + swap(pass_l, 2).astype(f32)
+    end_r = own_r + swap(pass_r, 1).astype(f32)
+    projected = jnp.concatenate([left, right, end_l, end_r], axis=1)
+    return (residual_in.astype(f32) + projected).astype(bf16)
 
 
 def on_device(
@@ -323,13 +398,13 @@
     blocks = channels // w_out.shape[0]
     square = lax.axis_size("tp") == 2 and count % inner == 0 and blocks % inner == 0
     if square:
-        half = w_out.shape[1] // 2
+        wide = 3 * w_out.shape[1] // 8
         lines = [list(range(start, count, inner)) for start in range(inner)]
         gather = functools.partial(
             lax.all_gather, axis_name="seq", axis=0, tiled=True, axis_index_groups=lines
         )
-        w_left = gather(w_out[:, :half])
-        w_right = gather(w_out[:, half:])
+        w_wide = gather(w_out[:, : 2 * wide])
+        w_last = gather(w_out[:, 2 * wide :])
     else:
         w_full = lax.all_gather(w_out, "seq", axis=0, tiled=True)
     tails = jnp.concatenate([features[:, rows - rim :], li_gates[:, rows - rim :]], axis=0)
@@ -344,12 +419,13 @@
     y_lo = medium(features, 0, mr_front[0], z_head, z_one, 0, medium_taps, short_mr, skip_mr)
     li_front = jnp.concatenate([fronts[3:], y_front[None]], axis=0)
     li_q, z_two, state_end = states(li_gates, y_lo, y_hi, li_front, short_li, poles)
-    incoming = carried_state(state_end, poles, rows)
+    prefix = square_state if square else carried_state
+    incoming = prefix(state_end, poles, rows)
     piece = w_out.shape[0]
     fan = inner if square else 1
     y_fan = long_out(z_two, li_q, incoming, poles, residues, skip_li[None], piece, fan)
     if square:
-        return project_square(residual_in, y_fan, w_left, w_right)
+        return project_square(residual_in, y_fan, w_wide, w_last)
     gathered = lax.all_gather(y_fan[0], "tp", axis=1, tiled=True)
     return (residual_in.astype(f32) + dot(gathered, w_full)).astype(bf16)
 

time: 462 us -> 415 us (0.90); the launches traced: 455 us -> 413 us
  starting transfers between devices: 126 us -> 85.2 us
  Pallas kernels: 104 us -> 143 us
  matrix products: 29.9 us -> 0 us
  waiting for transfers between devices: 165 us -> 141 us
  local copies, waits for them, and re-layouts: 6.05 us -> 15.2 us
  other arithmetic: 10 us -> 15.2 us
    pallas_call x0 -> x10, Pallas kernels: none -> 39.2 us  [product(): pl.pallas_call(product_kernel, grid=(columns // ct, row_blocks), in_specs...]
    ppermute x10 -> x6, starting transfers between devices: 86.8 us -> 48.9 us  [from_behind(): lax.ppermute(value, axis, [(source, source + steps) for source in range(c...]
    dot_general x5 -> x0, matrix products: 29.9 us -> none  [dot(): return jnp.dot(lhs, rhs, preferred_element_type=f32)]
    all_gather x2, waiting for transfers between devices: 60.1 us -> 40.5 us  [the longest x1 40.5 us: on_device(): w_last = gather(w_out[:, 2 * wide:])]
    ppermute x7 -> x14, waiting for transfers between devices: 79.4 us -> 62.8 us  [swap(): lax.ppermute(value, 'seq', [(source, source ^ bit) for source in range(co...]
    ppermute x10 -> x6, waiting for transfers between devices: 20.4 us -> 35.3 us  [from_behind(): lax.ppermute(value, axis, [(source, source + steps) for source in range(c...]
    unnamed x26 -> x36, local copies, waits for them, and re-layouts: 0.68 us -> 7.95 us
    ppermute x7 -> x14, starting transfers between devices: 39.6 us -> 36.2 us  [swap(): lax.ppermute(value, 'seq', [(source, source ^ bit) for source in range(co...]
  transfers between devices with their start and end apart: 20 -> 23, of which waited for: 12 -> 17; matrix products, arithmetic and copies ran while one was open for 8% -> 4% of each run, Pallas kernels for 23% -> 34%
where the time goes in v1:
time: 415 us; the launch traced here: 413 us
  Pallas kernels  143 us (34%)
  waiting for transfers between devices  141 us (34%)
  starting transfers between devices  85.2 us (21%)
  local copies, waits for them, and re-layouts  15.2 us (4%)
  other arithmetic  15.2 us (4%)
  between operations  14 us (3%)
    ppermute x14, waiting for transfers between devices, swap(): lax.ppermute(value, 'seq', [(source, source ^ bit) for source in range(co...  62.8 us
    pallas_call x2, Pallas kernels, medium(): pl.pallas_call(functools.partial(medium_kernel, width=channels // groups)...  53.6 us
    ppermute x6, starting transfers between devices, from_behind(): lax.ppermute(value, axis, [(source, source + steps) for source in range(c...  48.9 us
    all_gather x1, waiting for transfers between devices, on_device(): w_last = gather(w_out[:, 2 * wide:])  40.5 us
    pallas_call x10, Pallas kernels, product(): pl.pallas_call(product_kernel, grid=(columns // ct, row_blocks), in_specs...  39.2 us
    ppermute x14, starting transfers between devices, swap(): lax.ppermute(value, 'seq', [(source, source ^ bit) for source in range(co...  36.2 us
    ppermute x6, waiting for transfers between devices, from_behind(): lax.ppermute(value, axis, [(source, source + steps) for source in range(c...  35.3 us
    pallas_call x1, Pallas kernels, states(): pl.pallas_call(functools.partial(states_kernel, step=64), grid=(channels...  19.4 us
  transfers between devices with their start and end apart: 23, of which 17 were waited for; matrix products, arithmetic and copies ran while one was open for 4% of the time, Pallas kernels for 34%

profile of v1, /device:TPU:0, one launch (start us, length us, event | category | flops | bytes accessed | tf_op | source)
XLA Modules:
  0.0 413.4 jit_solution(3145042357846884159)
XLA Ops:
  6.5 3.7 slice.75
  11.3 4.9 %collective-permute-start = (bf16[5,8,4096]{2,1,0:T(8,128)(2,1)S(1)}, bf16[5,8,4096]{2,1,0:T(8,128)(2,1)S(1)}, u32[]{:S(2)}, u32[]{:S(2)}) collective-permute-start(bf16[5,8,4096]{2,1,0:T(8,128)(2,1)S(1)} %pad_maximum_fusion.3), channel_id=1, source_target_pairs={{0,2},{2,4},{4,6},{6,8},{8,10},{10,12},{12,14},{14,16},{16,18},{18... | collective-permute-start | bytes 983048 | tf_op jit(solution)/shard_map/ppermute | solution.py:17
  17.0 6.1 %collective-permute-done = bf16[5,8,4096]{2,1,0:T(8,128)(2,1)S(1)} collective-permute-done((bf16[5,8,4096]{2,1,0:T(8,128)(2,1)S(1)}, bf16[5,8,4096]{2,1,0:T(8,128)(2,1)S(1)}, u32[]{:S(2)}, u32[]{:S(2)}) %collective-permute-start) | collective-permute-done | bytes 327712 | tf_op jit(solution)/shard_map/ppermute | solution.py:17
  23.1 12.6 %gate.1.main_ref.head_ref = bf16[256,4096]{1,0:T(8,128)(2,1)S(1)} custom-call(bf16[3,256,4096]{2,1,0:T(8,128)(2,1)} %q_ref.3, bf16[3,256,4096]{2,1,0:T(8,128)(2,1)} %q_ref.3, f32[3,8,4096]{2,1,0:T(8,128)S(1)} %slice.90.front_ref, f32[3,7,4096]{2,1,0:T(8,128)S(1)} %copy-done.5), custom_call_target="tpu_custom_call" | custom-call | flops 62914560 | bytes 6291456 | tf_op jit(solution)/shard_map/gate/pallas_call | solution.py:148
  35.8 4.5 %collective-permute-start.1 = (bf16[128,4096]{1,0:T(8,128)(2,1)S(1)}, bf16[128,4096]{1,0:T(8,128)(2,1)S(1)}, u32[]{:S(2)}, u32[]{:S(2)}) collective-permute-start(bf16[128,4096]{1,0:T(8,128)(2,1)S(1)} %slice.91), channel_id=1, source_target_pairs={{0,2},{2,4},{4,6},{6,8},{8,10},{10,12},{12,14},{14,16},{16,18},{18... | collective-permute-start | bytes 3145736 | tf_op jit(solution)/shard_map/ppermute | solution.py:17
  40.3 26.8 %medium.3.yhi_ref = bf16[128,4096]{1,0:T(8,128)(2,1)S(1)} custom-call(bf16[3,256,4096]{2,1,0:T(8,128)(2,1)} %q_ref.3, f32[8,4096]{1,0:T(8,128)S(1)} %bitcast_convert_fusion.1.front_ref, bf16[256,4096]{1,0:T(8,128)(2,1)S(1)} %gate.1.main_ref.head_ref, bf16[256,4096]{1,0:T(8,128)(2,1)S(1)} %gate.1.main_ref.head_ref, bf16[128,256]{1,0:T(8,128)(2,1)S(1)} %copy-done.7, ...), custom_call_target="tpu_custom_call" | custom-call | flops 1310720000 | bytes 4194304 | tf_op jit(solution)/shard_map/medium/pallas_call | solution.py:171
  67.1 4.2 %collective-permute-start.2 = (bf16[8,4096]{1,0:T(8,128)(2,1)S(1)}, bf16[8,4096]{1,0:T(8,128)(2,1)S(1)}, u32[]{:S(2)}, u32[]{:S(2)}) collective-permute-start(bf16[8,4096]{1,0:T(8,128)(2,1)S(1)} %slice.93), channel_id=1, source_target_pairs={{0,2},{2,4},{4,6},{6,8},{8,10},{10,12},{12,14},{14,16},{16,18},{18... | collective-permute-start | bytes 196616 | tf_op jit(solution)/shard_map/ppermute | solution.py:17
  73.3 26.9 %medium.2.ylo_ref = bf16[128,4096]{1,0:T(8,128)(2,1)S(1)} custom-call(bf16[3,256,4096]{2,1,0:T(8,128)(2,1)} %q_ref.3, f32[8,4096]{1,0:T(8,128)S(1)} %slice_bitcast_fusion.front_ref, bf16[128,4096]{1,0:T(8,128)(2,1)S(1)} %collective-permute-done.1.head_ref, bf16[256,4096]{1,0:T(8,128)(2,1)S(1)} %gate.1.main_ref.head_ref, bf16[128,256]{1,0:T(8,128)(2,1)S(1)} %copy-done.7, ...), custom_call_target="tpu_custom_call" | custom-call | flops 1310720000 | bytes 4194304 | tf_op jit(solution)/shard_map/medium/pallas_call | solution.py:171
  100.2 19.4 %states.1 = (f32[256,4096]{1,0:T(8,128)}, f32[256,4096]{1,0:T(8,128)}, f32[16,4096]{1,0:T(8,128)S(1)}) custom-call(bf16[2,256,4096]{2,1,0:T(8,128)(2,1)} %g_ref.1, bf16[128,4096]{1,0:T(8,128)(2,1)S(1)} %medium.2.ylo_ref, bf16[128,4096]{1,0:T(8,128)(2,1)S(1)} %medium.3.yhi_ref, f32[3,8,4096]{2,1,0:T(8,128)S(1)} %pad_maximum_fusion.2.front_ref, ...), custom_call_target="tpu_custom_call" | custom-call | flops 104857600 | bytes 14680064 | tf_op jit(solution)/shard_map/states/pallas_call | solution.py:199
  121.9 17.6 %collective-permute-start.4 = (f32[16,4096]{1,0:T(8,128)S(1)}, f32[16,4096]{1,0:T(8,128)S(1)}, u32[]{:S(2)}, u32[]{:S(2)}) collective-permute-start(f32[16,4096]{1,0:T(8,128)S(1)} %get-tuple-element.10), channel_id=1, source_target_pairs={{0,4},{2,6},{4,0},{6,2},{8,12},{10,14},{12,8},{14,10},{16,20},{18,... | collective-permute-start | bytes 786440 | tf_op jit(solution)/shard_map/ppermute | solution.py:274
  139.5 9.9 %collective-permute-done.4 = f32[16,4096]{1,0:T(8,128)S(1)} collective-permute-done((f32[16,4096]{1,0:T(8,128)S(1)}, f32[16,4096]{1,0:T(8,128)S(1)}, u32[]{:S(2)}, u32[]{:S(2)}) %collective-permute-start.4) | collective-permute-done | bytes 262176 | tf_op jit(solution)/shard_map/ppermute | solution.py:274
  149.7 29.1 %collective-permute-start.6 = (f32[16,4096]{1,0:T(8,128)S(1)}, f32[16,4096]{1,0:T(8,128)S(1)}, u32[]{:S(2)}, u32[]{:S(2)}) collective-permute-start(f32[16,4096]{1,0:T(8,128)S(1)} %multiply_add_fusion.1), channel_id=1, source_target_pairs={{0,8},{2,10},{4,12},{6,14},{8,16},{10,18},{12,20},{14,22},{16,24},... | collective-permute-start | bytes 786440 | tf_op jit(solution)/shard_map/ppermute | solution.py:17
  178.8 4.8 %collective-permute-start.7 = (f32[16,4096]{1,0:T(8,128)S(1)}, f32[16,4096]{1,0:T(8,128)S(1)}, u32[]{:S(2)}, u32[]{:S(2)}) collective-permute-start(f32[16,4096]{1,0:T(8,128)S(1)} %multiply_add_fusion.1), channel_id=1, source_target_pairs={{0,16},{2,18},{4,20},{6,22},{8,24},{10,26},{12,28},{14,30},{1,17},... | collective-permute-start | bytes 786440 | tf_op jit(solution)/shard_map/ppermute | solution.py:17
  185.1 5.9 %collective-permute-done.6 = f32[16,4096]{1,0:T(8,128)S(1)} collective-permute-done((f32[16,4096]{1,0:T(8,128)S(1)}, f32[16,4096]{1,0:T(8,128)S(1)}, u32[]{:S(2)}, u32[]{:S(2)}) %collective-permute-start.6) | collective-permute-done | bytes 262176 | tf_op jit(solution)/shard_map/ppermute | solution.py:17
  191.0 11.2 %collective-permute-done.7 = f32[16,4096]{1,0:T(8,128)S(1)} collective-permute-done((f32[16,4096]{1,0:T(8,128)S(1)}, f32[16,4096]{1,0:T(8,128)S(1)}, u32[]{:S(2)}, u32[]{:S(2)}) %collective-permute-start.7) | collective-permute-done | bytes 262176 | tf_op jit(solution)/shard_map/ppermute | solution.py:17
  202.3 10.4 %collective-permute-done.8 = f32[16,4096]{1,0:T(8,128)S(1)} collective-permute-done((f32[16,4096]{1,0:T(8,128)S(1)}, f32[16,4096]{1,0:T(8,128)S(1)}, u32[]{:S(2)}, u32[]{:S(2)}) %collective-permute-start.8) | collective-permute-done | bytes 262176 | tf_op jit(solution)/shard_map/ppermute | solution.py:17
  213.0 18.4 %long.1 = bf16[4,256,1024]{2,1,0:T(8,128)(2,1)S(1)} custom-call(f32[256,4096]{1,0:T(8,128)} %get-tuple-element.8.z_ref, f32[256,4096]{1,0:T(8,128)} %get-tuple-element.9.q_ref, f32[16,4096]{1,0:T(8,128)S(1)} %multiply_add_fusion.in_ref, f32[16,4096]{1,0:T(8,128)S(1)} %copy-done.4, f32[16,4096]{1,0:T(8,128)S(1)} %copy-done.8, f32[1,4096]{1,0:T(1,128)S(1)} %bitcast.20), custom_call_target="tpu_custom_call" | custom-call | flops 104857600 | bytes 10485760 | tf_op jit(solution)/shard_map/long/pallas_call | solution.py:231
  235.1 12.3 %collective-permute-done.10 = bf16[256,1024]{1,0:T(8,128)(2,1)S(1)} collective-permute-done((bf16[256,1024]{1,0:T(8,128)(2,1)S(1)}, bf16[256,1024]{1,0:T(8,128)(2,1)S(1)}, u32[]{:S(2)}, u32[]{:S(2)}) %collective-permute-start.10) | collective-permute-done | bytes 524320 | tf_op jit(solution)/shard_map/ppermute | solution.py:274
  247.4 7.7 %collective-permute-done.11 = bf16[256,1024]{1,0:T(8,128)(2,1)S(1)} collective-permute-done((bf16[256,1024]{1,0:T(8,128)(2,1)S(1)}, bf16[256,1024]{1,0:T(8,128)(2,1)S(1)}, u32[]{:S(2)}, u32[]{:S(2)}) %collective-permute-start.11) | collective-permute-done | bytes 524320 | tf_op jit(solution)/shard_map/ppermute | solution.py:274
  261.6 2.5 broadcast_select_fusion.1
  268.7 7.7 %product.11 = bf16[512,1536]{1,0:T(8,128)(2,1)S(1)} custom-call(bf16[1024,2048]{1,0:T(8,128)(2,1)S(1)} %copy-done, bf16[2048,3072]{1,0:T(8,128)(2,1)} %all-gather.3.cloned.1.call-done.w_ref), custom_call_target="tpu_custom_call" | custom-call | flops 3221225472 | bytes 6291456 | tf_op jit(solution)/shard_map/product/pallas_call | solution.py:314
  276.8 7.7 %product.13 = bf16[512,1536]{1,0:T(8,128)(2,1)S(1)} custom-call(bf16[1024,2048]{1,0:T(8,128)(2,1)S(1)} %copy-done, bf16[2048,3072]{1,0:T(8,128)(2,1)} %all-gather.3.cloned.1.call-done.w_ref), custom_call_target="tpu_custom_call" | custom-call | flops 3221225472 | bytes 6291456 | tf_op jit(solution)/shard_map/product/pallas_call | solution.py:314
  284.5 4.1 collective-permute-start.15
  288.6 4.8 %product.14 = f32[256,1536]{1,0:T(8,128)S(1)} custom-call(bf16[1024,2048]{1,0:T(8,128)(2,1)S(1)} %copy-done, bf16[2048,3072]{1,0:T(8,128)(2,1)} %all-gather.3.cloned.1.call-done.w_ref), custom_call_target="tpu_custom_call" | custom-call | flops 1610612736 | bytes 6291456 | tf_op jit(solution)/shard_map/product/pallas_call | solution.py:314
  293.4 8.0 %product.10 = f32[512,1536]{1,0:T(8,128)S(1)} custom-call(bf16[1024,2048]{1,0:T(8,128)(2,1)S(1)} %copy-done, bf16[2048,3072]{1,0:T(8,128)(2,1)} %all-gather.3.cloned.1.call-done.w_ref), custom_call_target="tpu_custom_call" | custom-call | flops 3221225472 | bytes 6291456 | tf_op jit(solution)/shard_map/product/pallas_call | solution.py:314
  301.4 11.4 %collective-permute-done.13 = bf16[512,1536]{1,0:T(8,128)(2,1)S(1)} collective-permute-done((bf16[512,1536]{1,0:T(8,128)(2,1)S(1)}, bf16[512,1536]{1,0:T(8,128)(2,1)S(1)}, u32[]{:S(2)}, u32[]{:S(2)}) %collective-permute-start.13) | collective-permute-done | bytes 1572896 | tf_op jit(solution)/shard_map/ppermute | solution.py:274
  314.6 2.4 collective-permute-start.14
  317.0 6.9 %collective-permute-done.15 = bf16[512,1536]{1,0:T(8,128)(2,1)S(1)} collective-permute-done((bf16[512,1536]{1,0:T(8,128)(2,1)S(1)}, bf16[512,1536]{1,0:T(8,128)(2,1)S(1)}, u32[]{:S(2)}, u32[]{:S(2)}) %collective-permute-start.15) | collective-permute-done | bytes 1572896 | tf_op jit(solution)/shard_map/ppermute | solution.py:274
  326.3 40.5 %all-gather.5.cloned.1.call-done.w_ref = bf16[2048,1024]{1,0:T(8,128)(2,1)} async-done(((bf16[512,1024]{1,0:T(8,128)(2,1)}), bf16[2048,1024]{1,0:T(8,128)(2,1)}) %all-gather.5.cloned.1.call-update) | async-done | bytes 4194320 | tf_op jit(solution)/shard_map/all_gather | solution.py:407
  374.1 4.9 %product.12 = f32[256,1536]{1,0:T(8,128)S(1)} custom-call(bf16[1024,2048]{1,0:T(8,128)(2,1)S(1)} %copy-done.1, bf16[2048,3072]{1,0:T(8,128)(2,1)} %all-gather.3.cloned.1.call-done.w_ref), custom_call_target="tpu_custom_call" | custom-call | flops 1610612736 | bytes 6291456 | tf_op jit(solution)/shard_map/product/pallas_call | solution.py:314
  387.0 7.4 %collective-permute-done.17 = bf16[512,512]{1,0:T(8,128)(2,1)S(1)} collective-permute-done((bf16[512,512]{1,0:T(8,128)(2,1)S(1)}, bf16[512,512]{1,0:T(8,128)(2,1)S(1)}, u32[]{:S(2)}, u32[]{:S(2)}) %collective-permute-start.17) | collective-permute-done | bytes 524320 | tf_op jit(solution)/shard_map/ppermute | solution.py:274
  399.5 3.4 collective-permute-done.18
  (102 shorter events, 51.5 us)
Async XLA Ops:
  6.5 259.9 %all-gather.3.cloned.1.call-start = ((), (), s32[]{:S(2)}) async-start(), calls=%async_computation | async-start | bytes 15728640 | tf_op jit(solution)/shard_map/all_gather | solution.py:406
  10.3 12.9 %copy-start.5 = (f32[3,7,4096]{2,1,0:T(8,128)S(1)}, f32[3,7,4096]{2,1,0:T(8,128)}, u32[]{:S(2)}) copy-start(f32[3,7,4096]{2,1,0:T(8,128)} %taps_ref.6) | copy-start | bytes 1032196
  10.3 356.4 %all-gather.5.cloned.1.call-start = ((), (), s32[]{:S(2)}) async-start(), calls=%async_computation.1 | async-start | bytes 5242880 | tf_op jit(solution)/shard_map/all_gather | solution.py:407
  11.3 11.8 %collective-permute-start = (bf16[5,8,4096]{2,1,0:T(8,128)(2,1)S(1)}, bf16[5,8,4096]{2,1,0:T(8,128)(2,1)S(1)}, u32[]{:S(2)}, u32[]{:S(2)}) collective-permute-start(bf16[5,8,4096]{2,1,0:T(8,128)(2,1)S(1)} %pad_maximum_fusion.3), channel_id=1, source_target_pairs={{0,2},{2,4},{4,6},{6,8},{8,10},{10,12},{12,14},{14,16},{16,18},{18... | collective-permute-start | bytes 983048 | tf_op jit(solution)/shard_map/ppermute | solution.py:17
  35.8 37.4 %collective-permute-start.1 = (bf16[128,4096]{1,0:T(8,128)(2,1)S(1)}, bf16[128,4096]{1,0:T(8,128)(2,1)S(1)}, u32[]{:S(2)}, u32[]{:S(2)}) collective-permute-start(bf16[128,4096]{1,0:T(8,128)(2,1)S(1)} %slice.91), channel_id=1, source_target_pairs={{0,2},{2,4},{4,6},{6,8},{8,10},{10,12},{12,14},{14,16},{16,18},{18... | collective-permute-start | bytes 3145736 | tf_op jit(solution)/shard_map/ppermute | solution.py:17
  67.1 6.1 %collective-permute-start.2 = (bf16[8,4096]{1,0:T(8,128)(2,1)S(1)}, bf16[8,4096]{1,0:T(8,128)(2,1)S(1)}, u32[]{:S(2)}, u32[]{:S(2)}) collective-permute-start(bf16[8,4096]{1,0:T(8,128)(2,1)S(1)} %slice.93), channel_id=1, source_target_pairs={{0,2},{2,4},{4,6},{6,8},{8,10},{10,12},{12,14},{14,16},{16,18},{18... | collective-permute-start | bytes 196616 | tf_op jit(solution)/shard_map/ppermute | solution.py:17
  73.2 26.9 %copy-start.4 = (f32[16,4096]{1,0:T(8,128)S(1)}, f32[16,4096]{1,0:T(8,128)}, u32[]{:S(2)}) copy-start(f32[16,4096]{1,0:T(8,128)} %poles_ref.3) | copy-start | bytes 786436
  73.2 26.9 %copy-start.6 = (f32[3,7,4096]{2,1,0:T(8,128)S(1)}, f32[3,7,4096]{2,1,0:T(8,128)}, u32[]{:S(2)}) copy-start(f32[3,7,4096]{2,1,0:T(8,128)} %taps_ref.7) | copy-start | bytes 1032196
  119.6 93.3 %copy-start.8 = (f32[16,4096]{1,0:T(8,128)S(1)}, f32[16,4096]{1,0:T(8,128)}, u32[]{:S(2)}) copy-start(f32[16,4096]{1,0:T(8,128)} %res_ref.1) | copy-start | bytes 786436
  119.6 93.4 %copy-start.10 = (f32[4096]{0:T(1024)S(1)}, f32[4096]{0:T(1024)}, u32[]{:S(2)}) copy-start(f32[4096]{0:T(1024)} %param.20) | copy-start | bytes 49156
  119.6 19.9 %collective-permute-start.3 = (f32[16,4096]{1,0:T(8,128)S(1)}, f32[16,4096]{1,0:T(8,128)S(1)}, u32[]{:S(2)}, u32[]{:S(2)}) collective-permute-start(f32[16,4096]{1,0:T(8,128)S(1)} %get-tuple-element.10), channel_id=1, source_target_pairs={{0,2},{2,0},{4,6},{6,4},{8,10},{10,8},{12,14},{14,12},{16,18},{18,... | collective-permute-start | bytes 786440 | tf_op jit(solution)/shard_map/ppermute | solution.py:274
  121.9 27.5 %collective-permute-start.4 = (f32[16,4096]{1,0:T(8,128)S(1)}, f32[16,4096]{1,0:T(8,128)S(1)}, u32[]{:S(2)}, u32[]{:S(2)}) collective-permute-start(f32[16,4096]{1,0:T(8,128)S(1)} %get-tuple-element.10), channel_id=1, source_target_pairs={{0,4},{2,6},{4,0},{6,2},{8,12},{10,14},{12,8},{14,10},{16,20},{18,... | collective-permute-start | bytes 786440 | tf_op jit(solution)/shard_map/ppermute | solution.py:274
  139.5 10.0 %collective-permute-start.5 = (f32[16,4096]{1,0:T(8,128)S(1)}, f32[16,4096]{1,0:T(8,128)S(1)}, u32[]{:S(2)}, u32[]{:S(2)}) collective-permute-start(f32[16,4096]{1,0:T(8,128)S(1)} %get-tuple-element.10), channel_id=1, source_target_pairs={{0,6},{2,4},{4,2},{6,0},{8,14},{10,12},{12,10},{14,8},{16,22},{18,... | collective-permute-start | bytes 786440 | tf_op jit(solution)/shard_map/ppermute | solution.py:274
  149.7 41.3 %collective-permute-start.6 = (f32[16,4096]{1,0:T(8,128)S(1)}, f32[16,4096]{1,0:T(8,128)S(1)}, u32[]{:S(2)}, u32[]{:S(2)}) collective-permute-start(f32[16,4096]{1,0:T(8,128)S(1)} %multiply_add_fusion.1), channel_id=1, source_target_pairs={{0,8},{2,10},{4,12},{6,14},{8,16},{10,18},{12,20},{14,22},{16,24},... | collective-permute-start | bytes 786440 | tf_op jit(solution)/shard_map/ppermute | solution.py:17
  178.8 23.5 %collective-permute-start.7 = (f32[16,4096]{1,0:T(8,128)S(1)}, f32[16,4096]{1,0:T(8,128)S(1)}, u32[]{:S(2)}, u32[]{:S(2)}) collective-permute-start(f32[16,4096]{1,0:T(8,128)S(1)} %multiply_add_fusion.1), channel_id=1, source_target_pairs={{0,16},{2,18},{4,20},{6,22},{8,24},{10,26},{12,28},{14,30},{1,17},... | collective-permute-start | bytes 786440 | tf_op jit(solution)/shard_map/ppermute | solution.py:17
  183.6 29.0 %collective-permute-start.8 = (f32[16,4096]{1,0:T(8,128)S(1)}, f32[16,4096]{1,0:T(8,128)S(1)}, u32[]{:S(2)}, u32[]{:S(2)}) collective-permute-start(f32[16,4096]{1,0:T(8,128)S(1)} %multiply_add_fusion.1), channel_id=1, source_target_pairs={{0,24},{2,26},{4,28},{6,30},{1,25},{3,27},{5,29},{7,31}} | collective-permute-start | bytes 786440 | tf_op jit(solution)/shard_map/ppermute | solution.py:17
  231.6 15.8 %collective-permute-start.10 = (bf16[256,1024]{1,0:T(8,128)(2,1)S(1)}, bf16[256,1024]{1,0:T(8,128)(2,1)S(1)}, u32[]{:S(2)}, u32[]{:S(2)}) collective-permute-start(bf16[256,1024]{1,0:T(8,128)(2,1)S(1)} %get-tuple-element.16), channel_id=1, source_target_pairs={{0,6},{2,4},{4,2},{6,0},{8,14},{10,12},{12,10},{14,8},{16,22},{18,... | collective-permute-start | bytes 1572872 | tf_op jit(solution)/shard_map/ppermute | solution.py:274
  233.3 21.7 %collective-permute-start.11 = (bf16[256,1024]{1,0:T(8,128)(2,1)S(1)}, bf16[256,1024]{1,0:T(8,128)(2,1)S(1)}, u32[]{:S(2)}, u32[]{:S(2)}) collective-permute-start(bf16[256,1024]{1,0:T(8,128)(2,1)S(1)} %get-tuple-element.15), channel_id=1, source_target_pairs={{0,4},{2,6},{4,0},{6,2},{8,12},{10,14},{12,8},{14,10},{16,20},{18,... | collective-permute-start | bytes 1572872 | tf_op jit(solution)/shard_map/ppermute | solution.py:274
  234.6 22.0 %collective-permute-start.9 = (bf16[256,1024]{1,0:T(8,128)(2,1)S(1)}, bf16[256,1024]{1,0:T(8,128)(2,1)S(1)}, u32[]{:S(2)}, u32[]{:S(2)}) collective-permute-start(bf16[256,1024]{1,0:T(8,128)(2,1)S(1)} %get-tuple-element.13), channel_id=1, source_target_pairs={{0,2},{2,0},{4,6},{6,4},{8,10},{10,8},{12,14},{14,12},{16,18},{18,... | collective-permute-start | bytes 1572872 | tf_op jit(solution)/shard_map/ppermute | solution.py:274
  257.3 4.3 %collective-permute-start.12 = (bf16[1024,1024]{1,0:T(8,128)(2,1)S(1)}, bf16[1024,1024]{1,0:T(8,128)(2,1)}, u32[]{:S(2)}, u32[]{:S(2)}) collective-permute-start(bf16[1024,1024]{1,0:T(8,128)(2,1)S(1)} %pad_maximum_fusion.1), channel_id=1, source_target_pairs={{0,1},{1,0},{2,3},{3,2},{4,5},{5,4},{6,7},{7,6},{8,9},{9,8},{10,11... | collective-permute-start | bytes 6291464 | tf_op jit(solution)/shard_map/ppermute | solution.py:339
  276.4 36.5 %collective-permute-start.13 = (bf16[512,1536]{1,0:T(8,128)(2,1)S(1)}, bf16[512,1536]{1,0:T(8,128)(2,1)S(1)}, u32[]{:S(2)}, u32[]{:S(2)}) collective-permute-start(bf16[512,1536]{1,0:T(8,128)(2,1)S(1)} %product.11), channel_id=1, source_target_pairs={{0,2},{2,0},{4,6},{6,4},{8,10},{10,8},{12,14},{14,12},{16,18},{18,... | collective-permute-start | bytes 4718600 | tf_op jit(solution)/shard_map/ppermute | solution.py:274
  284.5 39.4 %collective-permute-start.15 = (bf16[512,1536]{1,0:T(8,128)(2,1)S(1)}, bf16[512,1536]{1,0:T(8,128)(2,1)S(1)}, u32[]{:S(2)}, u32[]{:S(2)}) collective-permute-start(bf16[512,1536]{1,0:T(8,128)(2,1)S(1)} %product.13), channel_id=1, source_target_pairs={{0,4},{2,6},{4,0},{6,2},{8,12},{10,14},{12,8},{14,10},{16,20},{18,... | collective-permute-start | bytes 4718600 | tf_op jit(solution)/shard_map/ppermute | solution.py:274
  314.6 64.5 %collective-permute-start.14 = (bf16[256,1536]{1,0:T(8,128)(2,1)}, bf16[256,1536]{1,0:T(8,128)(2,1)}, u32[]{:S(2)}, u32[]{:S(2)}) collective-permute-start(bf16[256,1536]{1,0:T(8,128)(2,1)} %fusion.3), channel_id=1, source_target_pairs={{0,4},{2,6},{4,0},{6,2},{8,12},{10,14},{12,8},{14,10},{16,20},{18,... | collective-permute-start | bytes 2359304 | tf_op jit(solution)/shard_map/ppermute | solution.py:274
  326.2 52.8 %collective-permute-start.16 = (bf16[256,1536]{1,0:T(8,128)(2,1)}, bf16[256,1536]{1,0:T(8,128)(2,1)}, u32[]{:S(2)}, u32[]{:S(2)}) collective-permute-start(bf16[256,1536]{1,0:T(8,128)(2,1)} %fusion.1), channel_id=1, source_target_pairs={{0,2},{2,0},{4,6},{6,4},{8,10},{10,8},{12,14},{14,12},{16,18},{18,... | collective-permute-start | bytes 2359304 | tf_op jit(solution)/shard_map/ppermute | solution.py:274
  374.1 4.9 %copy-start.3 = (bf16[2048,1024]{1,0:T(8,128)(2,1)S(1)}, bf16[2048,1024]{1,0:T(8,128)(2,1)}, u32[]{:S(2)}) copy-start(bf16[2048,1024]{1,0:T(8,128)(2,1)} %all-gather.5.cloned.1.call-done.w_ref) | copy-start | bytes 12582916
  380.7 4.7 %copy-start.14 = (f32[512,1536]{1,0:T(8,128)S(1)}, f32[512,1536]{1,0:T(8,128)}, u32[]{:S(2)}) copy-start(f32[512,1536]{1,0:T(8,128)} %copy-done.13) | copy-start | bytes 9437188
  380.7 13.7 %collective-permute-start.17 = (bf16[512,512]{1,0:T(8,128)(2,1)S(1)}, bf16[512,512]{1,0:T(8,128)(2,1)S(1)}, u32[]{:S(2)}, u32[]{:S(2)}) collective-permute-start(bf16[512,512]{1,0:T(8,128)(2,1)S(1)} %product.16), channel_id=1, source_target_pairs={{0,2},{2,0},{4,6},{6,4},{8,10},{10,8},{12,14},{14,12},{16,18},{18,... | collective-permute-start | bytes 1572872 | tf_op jit(solution)/shard_map/ppermute | solution.py:274
  383.8 14.3 %collective-permute-start.19 = (bf16[512,512]{1,0:T(8,128)(2,1)S(1)}, bf16[512,512]{1,0:T(8,128)(2,1)S(1)}, u32[]{:S(2)}, u32[]{:S(2)}) collective-permute-start(bf16[512,512]{1,0:T(8,128)(2,1)S(1)} %product.18), channel_id=1, source_target_pairs={{0,4},{2,6},{4,0},{6,2},{8,12},{10,14},{12,8},{14,10},{16,20},{18,... | collective-permute-start | bytes 1572872 | tf_op jit(solution)/shard_map/ppermute | solution.py:274
  385.4 10.8 %copy-start.12 = (f32[512,1536]{1,0:T(8,128)S(1)}, f32[512,1536]{1,0:T(8,128)}, u32[]{:S(2)}) copy-start(f32[512,1536]{1,0:T(8,128)} %copy-done.11) | copy-start | bytes 9437188
  394.6 8.2 %collective-permute-start.18 = (bf16[256,512]{1,0:T(8,128)(2,1)S(1)}, bf16[256,512]{1,0:T(8,128)(2,1)S(1)}, u32[]{:S(2)}, u32[]{:S(2)}) collective-permute-start(bf16[256,512]{1,0:T(8,128)(2,1)S(1)} %fusion.7), channel_id=1, source_target_pairs={{0,4},{2,6},{4,0},{6,2},{8,12},{10,14},{12,8},{14,10},{16,20},{18,... | collective-permute-start | bytes 786440 | tf_op jit(solution)/shard_map/ppermute | solution.py:274
  398.4 6.6 %copy-start.15 = (bf16[256,4096]{1,0:T(8,128)(2,1)S(1)}, bf16[256,4096]{1,0:T(8,128)(2,1)}, u32[]{:S(2)}) copy-start(bf16[256,4096]{1,0:T(8,128)(2,1)} %param.11) | copy-start | bytes 6291460
  398.4 6.4 %collective-permute-start.20 = (bf16[256,512]{1,0:T(8,128)(2,1)S(1)}, bf16[256,512]{1,0:T(8,128)(2,1)S(1)}, u32[]{:S(2)}, u32[]{:S(2)}) collective-permute-start(bf16[256,512]{1,0:T(8,128)(2,1)S(1)} %fusion.5), channel_id=1, source_target_pairs={{0,2},{2,0},{4,6},{6,4},{8,10},{10,8},{12,14},{14,12},{16,18},{18,... | collective-permute-start | bytes 786440 | tf_op jit(solution)/shard_map/ppermute | solution.py:274
  (11 other events, 25.7 us)
Sparse Core Ops, SparseCore 0:
  10.4 233.4 all-gather.2
  259.7 106.9 all-gather.4

commit v2 on v1

--- a/solution.py
+++ b/solution.py
@@ -289,15 +289,25 @@
             ahead = place - 1 - source
             lag = (rows * jnp.maximum(ahead, 0)).astype(f32)
             inside = inside + jnp.where(ahead >= 0, jnp.exp(lag * log_poles) * state, 0.0)
+    if count == inner:
+        return inside
+    share = state_end.shape[1] // inner
+
+    def quarter(value):
+        return lax.dynamic_slice_in_dim(value, place * share, share, axis=1)
+
+    part, log_part = quarter(whole), quarter(log_poles)
     before = None
     for steps in range(1, count // inner):
-        term = from_behind(whole, "seq", steps * inner)
+        term = from_behind(part, "seq", steps * inner)
         if steps > 1:
-            term = jnp.exp((rows * inner * (steps - 1)) * log_poles) * term
+            term = jnp.exp((rows * inner * (steps - 1)) * log_part) * term
         before = term if before is None else before + term
-    if before is None:
-        return inside
-    return inside + jnp.exp((rows * place).astype(f32) * log_poles) * before
+    total = jnp.zeros_like(state_end)
+    for bit in range(inner):
+        piece = before if bit == 0 else swap(before, bit)
+        total = lax.dynamic_update_slice_in_dim(total, piece, (place ^ bit) * share, axis=1)
+    return inside + jnp.exp((rows * place).astype(f32) * log_poles) * total
 
 
 def product_kernel(x_ref, w_ref, *rest):

time: 415 us -> 389 us (0.937)
  waiting for transfers between devices: 141 us -> 106 us
  starting transfers between devices: 85.2 us -> 94.6 us
    ppermute x6, waiting for transfers between devices: 35.3 us -> 12.3 us  [from_behind(): lax.ppermute(value, axis, [(source, source + steps) for source in range(c...]
    all_gather x1, waiting for transfers between devices: 40.5 us -> 27.2 us  [on_device(): w_last = gather(w_out[:, 2 * wide:])]
    ppermute x14 -> x17, starting transfers between devices: 36.2 us -> 45.7 us  [swap(): lax.ppermute(value, 'seq', [(source, source ^ bit) for source in range(co...]
    ppermute x14 -> x17, waiting for transfers between devices: 62.8 us -> 64.5 us  [swap(): lax.ppermute(value, 'seq', [(source, source ^ bit) for source in range(co...]
  transfers between devices with their start and end apart: 23 -> 26, of which waited for: 17 -> 19; matrix products, arithmetic and copies ran while one was open for 4% -> 4% of each run, Pallas kernels for 34% -> 36%
where the time goes in v2:
time: 389 us; the launch traced here: 388 us
  Pallas kernels  143 us (37%)
  waiting for transfers between devices  106 us (27%)
  starting transfers between devices  94.6 us (24%)
  local copies, waits for them, and re-layouts  15.3 us (4%)
  other arithmetic  15 us (4%)
  between operations  14 us (4%)
    ppermute x17, waiting for transfers between devices, swap(): lax.ppermute(value, 'seq', [(source, source ^ bit) for source in range(co...  64.5 us
    pallas_call x2, Pallas kernels, medium(): pl.pallas_call(functools.partial(medium_kernel, width=channels // groups)...  53.6 us
    ppermute x6, starting transfers between devices, from_behind(): lax.ppermute(value, axis, [(source, source + steps) for source in range(c...  48.9 us
    ppermute x17, starting transfers between devices, swap(): lax.ppermute(value, 'seq', [(source, source ^ bit) for source in range(co...  45.7 us
    pallas_call x10, Pallas kernels, product(): pl.pallas_call(product_kernel, grid=(columns // ct, row_blocks), in_specs...  39.2 us
    all_gather x1, waiting for transfers between devices, on_device(): w_last = gather(w_out[:, 2 * wide:])  27.2 us
    pallas_call x1, Pallas kernels, states(): pl.pallas_call(functools.partial(states_kernel, step=64), grid=(channels...  19.4 us
    pallas_call x1, Pallas kernels, long_out(): pl.pallas_call(long_kernel, grid=(channels // piece,), in_specs=[pl.Block...  18.4 us
  transfers between devices with their start and end apart: 26, of which 19 were waited for; matrix products, arithmetic and copies ran while one was open for 4% of the time, Pallas kernels for 36%

profile of v2, /device:TPU:0, one launch (start us, length us, event | category | flops | bytes accessed | tf_op | source)
XLA Modules:
  0.0 388.1 jit_solution(7595655030509951018)
XLA Ops:
  6.5 3.7 slice.75
  11.3 4.9 %collective-permute-start = (bf16[5,8,4096]{2,1,0:T(8,128)(2,1)S(1)}, bf16[5,8,4096]{2,1,0:T(8,128)(2,1)S(1)}, u32[]{:S(2)}, u32[]{:S(2)}) collective-permute-start(bf16[5,8,4096]{2,1,0:T(8,128)(2,1)S(1)} %pad_maximum_fusion.3), channel_id=1, source_target_pairs={{0,2},{2,4},{4,6},{6,8},{8,10},{10,12},{12,14},{14,16},{16,18},{18... | collective-permute-start | bytes 983048 | tf_op jit(solution)/shard_map/ppermute | solution.py:17
  17.0 6.1 %collective-permute-done = bf16[5,8,4096]{2,1,0:T(8,128)(2,1)S(1)} collective-permute-done((bf16[5,8,4096]{2,1,0:T(8,128)(2,1)S(1)}, bf16[5,8,4096]{2,1,0:T(8,128)(2,1)S(1)}, u32[]{:S(2)}, u32[]{:S(2)}) %collective-permute-start) | collective-permute-done | bytes 327712 | tf_op jit(solution)/shard_map/ppermute | solution.py:17
  23.1 12.6 %gate.1.main_ref.head_ref = bf16[256,4096]{1,0:T(8,128)(2,1)S(1)} custom-call(bf16[3,256,4096]{2,1,0:T(8,128)(2,1)} %q_ref.3, bf16[3,256,4096]{2,1,0:T(8,128)(2,1)} %q_ref.3, f32[3,8,4096]{2,1,0:T(8,128)S(1)} %slice.90.front_ref, f32[3,7,4096]{2,1,0:T(8,128)S(1)} %copy-done.5), custom_call_target="tpu_custom_call" | custom-call | flops 62914560 | bytes 6291456 | tf_op jit(solution)/shard_map/gate/pallas_call | solution.py:148
  35.8 4.5 %collective-permute-start.1 = (bf16[128,4096]{1,0:T(8,128)(2,1)S(1)}, bf16[128,4096]{1,0:T(8,128)(2,1)S(1)}, u32[]{:S(2)}, u32[]{:S(2)}) collective-permute-start(bf16[128,4096]{1,0:T(8,128)(2,1)S(1)} %slice.91), channel_id=1, source_target_pairs={{0,2},{2,4},{4,6},{6,8},{8,10},{10,12},{12,14},{14,16},{16,18},{18... | collective-permute-start | bytes 3145736 | tf_op jit(solution)/shard_map/ppermute | solution.py:17
  40.3 26.8 %medium.3.yhi_ref = bf16[128,4096]{1,0:T(8,128)(2,1)S(1)} custom-call(bf16[3,256,4096]{2,1,0:T(8,128)(2,1)} %q_ref.3, f32[8,4096]{1,0:T(8,128)S(1)} %bitcast_convert_fusion.1.front_ref, bf16[256,4096]{1,0:T(8,128)(2,1)S(1)} %gate.1.main_ref.head_ref, bf16[256,4096]{1,0:T(8,128)(2,1)S(1)} %gate.1.main_ref.head_ref, bf16[128,256]{1,0:T(8,128)(2,1)S(1)} %copy-done.7, ...), custom_call_target="tpu_custom_call" | custom-call | flops 1310720000 | bytes 4194304 | tf_op jit(solution)/shard_map/medium/pallas_call | solution.py:171
  67.1 4.2 %collective-permute-start.2 = (bf16[8,4096]{1,0:T(8,128)(2,1)S(1)}, bf16[8,4096]{1,0:T(8,128)(2,1)S(1)}, u32[]{:S(2)}, u32[]{:S(2)}) collective-permute-start(bf16[8,4096]{1,0:T(8,128)(2,1)S(1)} %slice.93), channel_id=1, source_target_pairs={{0,2},{2,4},{4,6},{6,8},{8,10},{10,12},{12,14},{14,16},{16,18},{18... | collective-permute-start | bytes 196616 | tf_op jit(solution)/shard_map/ppermute | solution.py:17
  73.3 26.9 %medium.2.ylo_ref = bf16[128,4096]{1,0:T(8,128)(2,1)S(1)} custom-call(bf16[3,256,4096]{2,1,0:T(8,128)(2,1)} %q_ref.3, f32[8,4096]{1,0:T(8,128)S(1)} %slice_bitcast_fusion.front_ref, bf16[128,4096]{1,0:T(8,128)(2,1)S(1)} %collective-permute-done.1.head_ref, bf16[256,4096]{1,0:T(8,128)(2,1)S(1)} %gate.1.main_ref.head_ref, bf16[128,256]{1,0:T(8,128)(2,1)S(1)} %copy-done.7, ...), custom_call_target="tpu_custom_call" | custom-call | flops 1310720000 | bytes 4194304 | tf_op jit(solution)/shard_map/medium/pallas_call | solution.py:171
  100.2 19.4 %states.1 = (f32[256,4096]{1,0:T(8,128)}, f32[256,4096]{1,0:T(8,128)}, f32[16,4096]{1,0:T(8,128)S(1)}) custom-call(bf16[2,256,4096]{2,1,0:T(8,128)(2,1)} %g_ref.1, bf16[128,4096]{1,0:T(8,128)(2,1)S(1)} %medium.2.ylo_ref, bf16[128,4096]{1,0:T(8,128)(2,1)S(1)} %medium.3.yhi_ref, f32[3,8,4096]{2,1,0:T(8,128)S(1)} %pad_maximum_fusion.2.front_ref, ...), custom_call_target="tpu_custom_call" | custom-call | flops 104857600 | bytes 14680064 | tf_op jit(solution)/shard_map/states/pallas_call | solution.py:199
  119.6 2.3 collective-permute-start.3
  122.0 17.6 %collective-permute-start.4 = (f32[16,4096]{1,0:T(8,128)S(1)}, f32[16,4096]{1,0:T(8,128)S(1)}, u32[]{:S(2)}, u32[]{:S(2)}) collective-permute-start(f32[16,4096]{1,0:T(8,128)S(1)} %get-tuple-element.10), channel_id=1, source_target_pairs={{0,4},{2,6},{4,0},{6,2},{8,12},{10,14},{12,8},{14,10},{16,20},{18,... | collective-permute-start | bytes 786440 | tf_op jit(solution)/shard_map/ppermute | solution.py:274
  139.6 9.9 %collective-permute-done.4 = f32[16,4096]{1,0:T(8,128)S(1)} collective-permute-done((f32[16,4096]{1,0:T(8,128)S(1)}, f32[16,4096]{1,0:T(8,128)S(1)}, u32[]{:S(2)}, u32[]{:S(2)}) %collective-permute-start.4) | collective-permute-done | bytes 262176 | tf_op jit(solution)/shard_map/ppermute | solution.py:274
  149.5 29.1 %collective-permute-start.6 = (f32[16,1024]{1,0:T(8,128)S(1)}, f32[16,1024]{1,0:T(8,128)S(1)}, u32[]{:S(2)}, u32[]{:S(2)}) collective-permute-start(f32[16,1024]{1,0:T(8,128)S(1)} %fusion.9), channel_id=1, source_target_pairs={{0,8},{2,10},{4,12},{6,14},{8,16},{10,18},{12,20},{14,22},{16,24},... | collective-permute-start | bytes 196616 | tf_op jit(solution)/shard_map/ppermute | solution.py:17
  178.6 4.8 %collective-permute-start.7 = (f32[16,1024]{1,0:T(8,128)S(1)}, f32[16,1024]{1,0:T(8,128)S(1)}, u32[]{:S(2)}, u32[]{:S(2)}) collective-permute-start(f32[16,1024]{1,0:T(8,128)S(1)} %fusion.9), channel_id=1, source_target_pairs={{0,16},{2,18},{4,20},{6,22},{8,24},{10,26},{12,28},{14,30},{1,17},... | collective-permute-start | bytes 196616 | tf_op jit(solution)/shard_map/ppermute | solution.py:17
  185.0 2.3 collective-permute-done.7
  196.8 18.4 %long.1 = bf16[4,256,1024]{2,1,0:T(8,128)(2,1)S(1)} custom-call(f32[256,4096]{1,0:T(8,128)} %get-tuple-element.8.z_ref, f32[256,4096]{1,0:T(8,128)} %get-tuple-element.9.q_ref, f32[16,4096]{1,0:T(8,128)S(1)} %multiply_add_fusion.in_ref, f32[16,4096]{1,0:T(8,128)S(1)} %copy-done.4, f32[16,4096]{1,0:T(8,128)S(1)} %copy-done.8, f32[1,4096]{1,0:T(1,128)S(1)} %bitcast.20), custom_call_target="tpu_custom_call" | custom-call | flops 104857600 | bytes 10485760 | tf_op jit(solution)/shard_map/long/pallas_call | solution.py:231
  219.0 11.4 %collective-permute-done.12 = bf16[256,1024]{1,0:T(8,128)(2,1)S(1)} collective-permute-done((bf16[256,1024]{1,0:T(8,128)(2,1)S(1)}, bf16[256,1024]{1,0:T(8,128)(2,1)S(1)}, u32[]{:S(2)}, u32[]{:S(2)}) %collective-permute-start.12) | collective-permute-done | bytes 524320 | tf_op jit(solution)/shard_map/ppermute | solution.py:274
  230.3 9.4 %collective-permute-done.13 = bf16[256,1024]{1,0:T(8,128)(2,1)S(1)} collective-permute-done((bf16[256,1024]{1,0:T(8,128)(2,1)S(1)}, bf16[256,1024]{1,0:T(8,128)(2,1)S(1)}, u32[]{:S(2)}, u32[]{:S(2)}) %collective-permute-start.13) | collective-permute-done | bytes 524320 | tf_op jit(solution)/shard_map/ppermute | solution.py:274
  246.2 2.5 broadcast_select_fusion.1
  248.6 2.4 pad_maximum_fusion.x_ref
  253.3 7.7 %product.11 = bf16[512,1536]{1,0:T(8,128)(2,1)S(1)} custom-call(bf16[1024,2048]{1,0:T(8,128)(2,1)S(1)} %copy-done, bf16[2048,3072]{1,0:T(8,128)(2,1)} %all-gather.3.cloned.1.call-done.w_ref), custom_call_target="tpu_custom_call" | custom-call | flops 3221225472 | bytes 6291456 | tf_op jit(solution)/shard_map/product/pallas_call | solution.py:324
  261.4 7.9 %product.13 = bf16[512,1536]{1,0:T(8,128)(2,1)S(1)} custom-call(bf16[1024,2048]{1,0:T(8,128)(2,1)S(1)} %copy-done, bf16[2048,3072]{1,0:T(8,128)(2,1)} %all-gather.3.cloned.1.call-done.w_ref), custom_call_target="tpu_custom_call" | custom-call | flops 3221225472 | bytes 6291456 | tf_op jit(solution)/shard_map/product/pallas_call | solution.py:324
  269.3 7.1 %collective-permute-start.18 = (bf16[512,1536]{1,0:T(8,128)(2,1)S(1)}, bf16[512,1536]{1,0:T(8,128)(2,1)S(1)}, u32[]{:S(2)}, u32[]{:S(2)}) collective-permute-start(bf16[512,1536]{1,0:T(8,128)(2,1)S(1)} %product.13), channel_id=1, source_target_pairs={{0,4},{2,6},{4,0},{6,2},{8,12},{10,14},{12,8},{14,10},{16,20},{18,... | collective-permute-start | bytes 4718600 | tf_op jit(solution)/shard_map/ppermute | solution.py:274
  276.3 4.7 %product.14 = f32[256,1536]{1,0:T(8,128)S(1)} custom-call(bf16[1024,2048]{1,0:T(8,128)(2,1)S(1)} %copy-done, bf16[2048,3072]{1,0:T(8,128)(2,1)} %all-gather.3.cloned.1.call-done.w_ref), custom_call_target="tpu_custom_call" | custom-call | flops 1610612736 | bytes 6291456 | tf_op jit(solution)/shard_map/product/pallas_call | solution.py:324
  281.1 7.8 %product.10 = f32[512,1536]{1,0:T(8,128)S(1)} custom-call(bf16[1024,2048]{1,0:T(8,128)(2,1)S(1)} %copy-done, bf16[2048,3072]{1,0:T(8,128)(2,1)} %all-gather.3.cloned.1.call-done.w_ref), custom_call_target="tpu_custom_call" | custom-call | flops 3221225472 | bytes 6291456 | tf_op jit(solution)/shard_map/product/pallas_call | solution.py:324
  288.9 8.5 %collective-permute-done.16 = bf16[512,1536]{1,0:T(8,128)(2,1)S(1)} collective-permute-done((bf16[512,1536]{1,0:T(8,128)(2,1)S(1)}, bf16[512,1536]{1,0:T(8,128)(2,1)S(1)}, u32[]{:S(2)}, u32[]{:S(2)}) %collective-permute-start.16) | collective-permute-done | bytes 1572896 | tf_op jit(solution)/shard_map/ppermute | solution.py:274
  299.1 5.2 %collective-permute-start.17 = (bf16[256,1536]{1,0:T(8,128)(2,1)}, bf16[256,1536]{1,0:T(8,128)(2,1)}, u32[]{:S(2)}, u32[]{:S(2)}) collective-permute-start(bf16[256,1536]{1,0:T(8,128)(2,1)} %fusion.3), channel_id=1, source_target_pairs={{0,4},{2,6},{4,0},{6,2},{8,12},{10,14},{12,8},{14,10},{16,20},{18,... | collective-permute-start | bytes 2359304 | tf_op jit(solution)/shard_map/ppermute | solution.py:274
  304.4 7.2 %collective-permute-done.18 = bf16[512,1536]{1,0:T(8,128)(2,1)S(1)} collective-permute-done((bf16[512,1536]{1,0:T(8,128)(2,1)S(1)}, bf16[512,1536]{1,0:T(8,128)(2,1)S(1)}, u32[]{:S(2)}, u32[]{:S(2)}) %collective-permute-start.18) | collective-permute-done | bytes 1572896 | tf_op jit(solution)/shard_map/ppermute | solution.py:274
  314.0 27.2 %all-gather.5.cloned.1.call-done.w_ref = bf16[2048,1024]{1,0:T(8,128)(2,1)} async-done(((bf16[512,1024]{1,0:T(8,128)(2,1)}), bf16[2048,1024]{1,0:T(8,128)(2,1)}) %all-gather.5.cloned.1.call-update) | async-done | bytes 4194320 | tf_op jit(solution)/shard_map/all_gather | solution.py:417
  348.6 4.9 %product.12 = f32[256,1536]{1,0:T(8,128)S(1)} custom-call(bf16[1024,2048]{1,0:T(8,128)(2,1)S(1)} %copy-done.1, bf16[2048,3072]{1,0:T(8,128)(2,1)} %all-gather.3.cloned.1.call-done.w_ref), custom_call_target="tpu_custom_call" | custom-call | flops 1610612736 | bytes 6291456 | tf_op jit(solution)/shard_map/product/pallas_call | solution.py:324
  361.5 7.4 %collective-permute-done.20 = bf16[512,512]{1,0:T(8,128)(2,1)S(1)} collective-permute-done((bf16[512,512]{1,0:T(8,128)(2,1)S(1)}, bf16[512,512]{1,0:T(8,128)(2,1)S(1)}, u32[]{:S(2)}, u32[]{:S(2)}) %collective-permute-start.20) | collective-permute-done | bytes 524320 | tf_op jit(solution)/shard_map/ppermute | solution.py:274
  373.9 3.4 collective-permute-done.21
  (114 shorter events, 56.0 us)
Async XLA Ops:
  6.5 244.5 %all-gather.3.cloned.1.call-start = ((), (), s32[]{:S(2)}) async-start(), calls=%async_computation | async-start | bytes 15728640 | tf_op jit(solution)/shard_map/all_gather | solution.py:416
  10.3 12.9 %copy-start.5 = (f32[3,7,4096]{2,1,0:T(8,128)S(1)}, f32[3,7,4096]{2,1,0:T(8,128)}, u32[]{:S(2)}) copy-start(f32[3,7,4096]{2,1,0:T(8,128)} %taps_ref.6) | copy-start | bytes 1032196
  10.3 330.9 %all-gather.5.cloned.1.call-start = ((), (), s32[]{:S(2)}) async-start(), calls=%async_computation.1 | async-start | bytes 5242880 | tf_op jit(solution)/shard_map/all_gather | solution.py:417
  11.3 11.8 %collective-permute-start = (bf16[5,8,4096]{2,1,0:T(8,128)(2,1)S(1)}, bf16[5,8,4096]{2,1,0:T(8,128)(2,1)S(1)}, u32[]{:S(2)}, u32[]{:S(2)}) collective-permute-start(bf16[5,8,4096]{2,1,0:T(8,128)(2,1)S(1)} %pad_maximum_fusion.3), channel_id=1, source_target_pairs={{0,2},{2,4},{4,6},{6,8},{8,10},{10,12},{12,14},{14,16},{16,18},{18... | collective-permute-start | bytes 983048 | tf_op jit(solution)/shard_map/ppermute | solution.py:17
  35.8 37.4 %collective-permute-start.1 = (bf16[128,4096]{1,0:T(8,128)(2,1)S(1)}, bf16[128,4096]{1,0:T(8,128)(2,1)S(1)}, u32[]{:S(2)}, u32[]{:S(2)}) collective-permute-start(bf16[128,4096]{1,0:T(8,128)(2,1)S(1)} %slice.91), channel_id=1, source_target_pairs={{0,2},{2,4},{4,6},{6,8},{8,10},{10,12},{12,14},{14,16},{16,18},{18... | collective-permute-start | bytes 3145736 | tf_op jit(solution)/shard_map/ppermute | solution.py:17
  67.1 6.1 %collective-permute-start.2 = (bf16[8,4096]{1,0:T(8,128)(2,1)S(1)}, bf16[8,4096]{1,0:T(8,128)(2,1)S(1)}, u32[]{:S(2)}, u32[]{:S(2)}) collective-permute-start(bf16[8,4096]{1,0:T(8,128)(2,1)S(1)} %slice.93), channel_id=1, source_target_pairs={{0,2},{2,4},{4,6},{6,8},{8,10},{10,12},{12,14},{14,16},{16,18},{18... | collective-permute-start | bytes 196616 | tf_op jit(solution)/shard_map/ppermute | solution.py:17
  73.2 26.9 %copy-start.4 = (f32[16,4096]{1,0:T(8,128)S(1)}, f32[16,4096]{1,0:T(8,128)}, u32[]{:S(2)}) copy-start(f32[16,4096]{1,0:T(8,128)} %poles_ref.3) | copy-start | bytes 786436
  73.2 26.9 %copy-start.6 = (f32[3,7,4096]{2,1,0:T(8,128)S(1)}, f32[3,7,4096]{2,1,0:T(8,128)}, u32[]{:S(2)}) copy-start(f32[3,7,4096]{2,1,0:T(8,128)} %taps_ref.7) | copy-start | bytes 1032196
  119.6 77.2 %copy-start.8 = (f32[16,4096]{1,0:T(8,128)S(1)}, f32[16,4096]{1,0:T(8,128)}, u32[]{:S(2)}) copy-start(f32[16,4096]{1,0:T(8,128)} %res_ref.1) | copy-start | bytes 786436
  119.6 77.2 %copy-start.10 = (f32[4096]{0:T(1024)S(1)}, f32[4096]{0:T(1024)}, u32[]{:S(2)}) copy-start(f32[4096]{0:T(1024)} %param.20) | copy-start | bytes 49156
  119.6 20.0 %collective-permute-start.3 = (f32[16,4096]{1,0:T(8,128)S(1)}, f32[16,4096]{1,0:T(8,128)S(1)}, u32[]{:S(2)}, u32[]{:S(2)}) collective-permute-start(f32[16,4096]{1,0:T(8,128)S(1)} %get-tuple-element.10), channel_id=1, source_target_pairs={{0,2},{2,0},{4,6},{6,4},{8,10},{10,8},{12,14},{14,12},{16,18},{18,... | collective-permute-start | bytes 786440 | tf_op jit(solution)/shard_map/ppermute | solution.py:274
  122.0 27.5 %collective-permute-start.4 = (f32[16,4096]{1,0:T(8,128)S(1)}, f32[16,4096]{1,0:T(8,128)S(1)}, u32[]{:S(2)}, u32[]{:S(2)}) collective-permute-start(f32[16,4096]{1,0:T(8,128)S(1)} %get-tuple-element.10), channel_id=1, source_target_pairs={{0,4},{2,6},{4,0},{6,2},{8,12},{10,14},{12,8},{14,10},{16,20},{18,... | collective-permute-start | bytes 786440 | tf_op jit(solution)/shard_map/ppermute | solution.py:274
  139.5 10.0 %collective-permute-start.5 = (f32[16,4096]{1,0:T(8,128)S(1)}, f32[16,4096]{1,0:T(8,128)S(1)}, u32[]{:S(2)}, u32[]{:S(2)}) collective-permute-start(f32[16,4096]{1,0:T(8,128)S(1)} %get-tuple-element.10), channel_id=1, source_target_pairs={{0,6},{2,4},{4,2},{6,0},{8,14},{10,12},{12,10},{14,8},{16,22},{18,... | collective-permute-start | bytes 786440 | tf_op jit(solution)/shard_map/ppermute | solution.py:274
  149.5 35.4 %collective-permute-start.6 = (f32[16,1024]{1,0:T(8,128)S(1)}, f32[16,1024]{1,0:T(8,128)S(1)}, u32[]{:S(2)}, u32[]{:S(2)}) collective-permute-start(f32[16,1024]{1,0:T(8,128)S(1)} %fusion.9), channel_id=1, source_target_pairs={{0,8},{2,10},{4,12},{6,14},{8,16},{10,18},{12,20},{14,22},{16,24},... | collective-permute-start | bytes 196616 | tf_op jit(solution)/shard_map/ppermute | solution.py:17
  178.6 8.6 %collective-permute-start.7 = (f32[16,1024]{1,0:T(8,128)S(1)}, f32[16,1024]{1,0:T(8,128)S(1)}, u32[]{:S(2)}, u32[]{:S(2)}) collective-permute-start(f32[16,1024]{1,0:T(8,128)S(1)} %fusion.9), channel_id=1, source_target_pairs={{0,16},{2,18},{4,20},{6,22},{8,24},{10,26},{12,28},{14,30},{1,17},... | collective-permute-start | bytes 196616 | tf_op jit(solution)/shard_map/ppermute | solution.py:17
  183.5 6.0 %collective-permute-start.8 = (f32[16,1024]{1,0:T(8,128)S(1)}, f32[16,1024]{1,0:T(8,128)S(1)}, u32[]{:S(2)}, u32[]{:S(2)}) collective-permute-start(f32[16,1024]{1,0:T(8,128)S(1)} %fusion.9), channel_id=1, source_target_pairs={{0,24},{2,26},{4,28},{6,30},{1,25},{3,27},{5,29},{7,31}} | collective-permute-start | bytes 196616 | tf_op jit(solution)/shard_map/ppermute | solution.py:17
  189.5 5.0 %collective-permute-start.9 = (f32[16,1024]{1,0:T(8,128)S(1)}, f32[16,1024]{1,0:T(8,128)S(1)}, u32[]{:S(2)}, u32[]{:S(2)}) collective-permute-start(f32[16,1024]{1,0:T(8,128)S(1)} %get-tuple-element.12), channel_id=1, source_target_pairs={{0,2},{2,0},{4,6},{6,4},{8,10},{10,8},{12,14},{14,12},{16,18},{18,... | collective-permute-start | bytes 196616 | tf_op jit(solution)/shard_map/ppermute | solution.py:274
  191.3 4.3 %collective-permute-start.10 = (f32[16,1024]{1,0:T(8,128)S(1)}, f32[16,1024]{1,0:T(8,128)S(1)}, u32[]{:S(2)}, u32[]{:S(2)}) collective-permute-start(f32[16,1024]{1,0:T(8,128)S(1)} %get-tuple-element.12), channel_id=1, source_target_pairs={{0,4},{2,6},{4,0},{6,2},{8,12},{10,14},{12,8},{14,10},{16,20},{18,... | collective-permute-start | bytes 196616 | tf_op jit(solution)/shard_map/ppermute | solution.py:274
  191.3 5.2 %collective-permute-start.11 = (f32[16,1024]{1,0:T(8,128)S(1)}, f32[16,1024]{1,0:T(8,128)S(1)}, u32[]{:S(2)}, u32[]{:S(2)}) collective-permute-start(f32[16,1024]{1,0:T(8,128)S(1)} %get-tuple-element.12), channel_id=1, source_target_pairs={{0,6},{2,4},{4,2},{6,0},{8,14},{10,12},{12,10},{14,8},{16,22},{18,... | collective-permute-start | bytes 196616 | tf_op jit(solution)/shard_map/ppermute | solution.py:274
  215.4 14.9 %collective-permute-start.12 = (bf16[256,1024]{1,0:T(8,128)(2,1)S(1)}, bf16[256,1024]{1,0:T(8,128)(2,1)S(1)}, u32[]{:S(2)}, u32[]{:S(2)}) collective-permute-start(bf16[256,1024]{1,0:T(8,128)(2,1)S(1)} %get-tuple-element.15), channel_id=1, source_target_pairs={{0,2},{2,0},{4,6},{6,4},{8,10},{10,8},{12,14},{14,12},{16,18},{18,... | collective-permute-start | bytes 1572872 | tf_op jit(solution)/shard_map/ppermute | solution.py:274
  216.9 22.8 %collective-permute-start.13 = (bf16[256,1024]{1,0:T(8,128)(2,1)S(1)}, bf16[256,1024]{1,0:T(8,128)(2,1)S(1)}, u32[]{:S(2)}, u32[]{:S(2)}) collective-permute-start(bf16[256,1024]{1,0:T(8,128)(2,1)S(1)} %get-tuple-element.18), channel_id=1, source_target_pairs={{0,6},{2,4},{4,2},{6,0},{8,14},{10,12},{12,10},{14,8},{16,22},{18,... | collective-permute-start | bytes 1572872 | tf_op jit(solution)/shard_map/ppermute | solution.py:274
  218.9 22.2 %collective-permute-start.14 = (bf16[256,1024]{1,0:T(8,128)(2,1)S(1)}, bf16[256,1024]{1,0:T(8,128)(2,1)S(1)}, u32[]{:S(2)}, u32[]{:S(2)}) collective-permute-start(bf16[256,1024]{1,0:T(8,128)(2,1)S(1)} %get-tuple-element.17), channel_id=1, source_target_pairs={{0,4},{2,6},{4,0},{6,2},{8,12},{10,14},{12,8},{14,10},{16,20},{18,... | collective-permute-start | bytes 1572872 | tf_op jit(solution)/shard_map/ppermute | solution.py:274
  241.9 4.3 %collective-permute-start.15 = (bf16[1024,1024]{1,0:T(8,128)(2,1)S(1)}, bf16[1024,1024]{1,0:T(8,128)(2,1)}, u32[]{:S(2)}, u32[]{:S(2)}) collective-permute-start(bf16[1024,1024]{1,0:T(8,128)(2,1)S(1)} %pad_maximum_fusion.1), channel_id=1, source_target_pairs={{0,1},{1,0},{2,3},{3,2},{4,5},{5,4},{6,7},{7,6},{8,9},{9,8},{10,11... | collective-permute-start | bytes 6291464 | tf_op jit(solution)/shard_map/ppermute | solution.py:349
  260.9 36.5 %collective-permute-start.16 = (bf16[512,1536]{1,0:T(8,128)(2,1)S(1)}, bf16[512,1536]{1,0:T(8,128)(2,1)S(1)}, u32[]{:S(2)}, u32[]{:S(2)}) collective-permute-start(bf16[512,1536]{1,0:T(8,128)(2,1)S(1)} %product.11), channel_id=1, source_target_pairs={{0,2},{2,0},{4,6},{6,4},{8,10},{10,8},{12,14},{14,12},{16,18},{18,... | collective-permute-start | bytes 4718600 | tf_op jit(solution)/shard_map/ppermute | solution.py:274
  269.3 42.4 %collective-permute-start.18 = (bf16[512,1536]{1,0:T(8,128)(2,1)S(1)}, bf16[512,1536]{1,0:T(8,128)(2,1)S(1)}, u32[]{:S(2)}, u32[]{:S(2)}) collective-permute-start(bf16[512,1536]{1,0:T(8,128)(2,1)S(1)} %product.13), channel_id=1, source_target_pairs={{0,4},{2,6},{4,0},{6,2},{8,12},{10,14},{12,8},{14,10},{16,20},{18,... | collective-permute-start | bytes 4718600 | tf_op jit(solution)/shard_map/ppermute | solution.py:274
  299.1 54.3 %collective-permute-start.17 = (bf16[256,1536]{1,0:T(8,128)(2,1)}, bf16[256,1536]{1,0:T(8,128)(2,1)}, u32[]{:S(2)}, u32[]{:S(2)}) collective-permute-start(bf16[256,1536]{1,0:T(8,128)(2,1)} %fusion.3), channel_id=1, source_target_pairs={{0,4},{2,6},{4,0},{6,2},{8,12},{10,14},{12,8},{14,10},{16,20},{18,... | collective-permute-start | bytes 2359304 | tf_op jit(solution)/shard_map/ppermute | solution.py:274
  314.0 39.5 %collective-permute-start.19 = (bf16[256,1536]{1,0:T(8,128)(2,1)}, bf16[256,1536]{1,0:T(8,128)(2,1)}, u32[]{:S(2)}, u32[]{:S(2)}) collective-permute-start(bf16[256,1536]{1,0:T(8,128)(2,1)} %fusion.1), channel_id=1, source_target_pairs={{0,2},{2,0},{4,6},{6,4},{8,10},{10,8},{12,14},{14,12},{16,18},{18,... | collective-permute-start | bytes 2359304 | tf_op jit(solution)/shard_map/ppermute | solution.py:274
  355.1 13.8 %collective-permute-start.20 = (bf16[512,512]{1,0:T(8,128)(2,1)S(1)}, bf16[512,512]{1,0:T(8,128)(2,1)S(1)}, u32[]{:S(2)}, u32[]{:S(2)}) collective-permute-start(bf16[512,512]{1,0:T(8,128)(2,1)S(1)} %product.16), channel_id=1, source_target_pairs={{0,2},{2,0},{4,6},{6,4},{8,10},{10,8},{12,14},{14,12},{16,18},{18,... | collective-permute-start | bytes 1572872 | tf_op jit(solution)/shard_map/ppermute | solution.py:274
  358.3 14.3 %collective-permute-start.22 = (bf16[512,512]{1,0:T(8,128)(2,1)S(1)}, bf16[512,512]{1,0:T(8,128)(2,1)S(1)}, u32[]{:S(2)}, u32[]{:S(2)}) collective-permute-start(bf16[512,512]{1,0:T(8,128)(2,1)S(1)} %product.18), channel_id=1, source_target_pairs={{0,4},{2,6},{4,0},{6,2},{8,12},{10,14},{12,8},{14,10},{16,20},{18,... | collective-permute-start | bytes 1572872 | tf_op jit(solution)/shard_map/ppermute | solution.py:274
  359.8 11.0 %copy-start.12 = (f32[512,1536]{1,0:T(8,128)S(1)}, f32[512,1536]{1,0:T(8,128)}, u32[]{:S(2)}) copy-start(f32[512,1536]{1,0:T(8,128)} %copy-done.11) | copy-start | bytes 9437188
  369.1 8.2 %collective-permute-start.21 = (bf16[256,512]{1,0:T(8,128)(2,1)S(1)}, bf16[256,512]{1,0:T(8,128)(2,1)S(1)}, u32[]{:S(2)}, u32[]{:S(2)}) collective-permute-start(bf16[256,512]{1,0:T(8,128)(2,1)S(1)} %fusion.7), channel_id=1, source_target_pairs={{0,4},{2,6},{4,0},{6,2},{8,12},{10,14},{12,8},{14,10},{16,20},{18,... | collective-permute-start | bytes 786440 | tf_op jit(solution)/shard_map/ppermute | solution.py:274
  372.9 6.7 %collective-permute-start.23 = (bf16[256,512]{1,0:T(8,128)(2,1)S(1)}, bf16[256,512]{1,0:T(8,128)(2,1)S(1)}, u32[]{:S(2)}, u32[]{:S(2)}) collective-permute-start(bf16[256,512]{1,0:T(8,128)(2,1)S(1)} %fusion.5), channel_id=1, source_target_pairs={{0,2},{2,0},{4,6},{6,4},{8,10},{10,8},{12,14},{14,12},{16,18},{18,... | collective-permute-start | bytes 786440 | tf_op jit(solution)/shard_map/ppermute | solution.py:274
  (14 other events, 44.9 us)
Sparse Core Ops, SparseCore 0:
  10.4 220.8 all-gather.2
  244.3 96.8 all-gather.4
